TPU v7x, 32 devices: a whole 2x2x4 slice. The times are simulated.
32 devices in a mesh: dp: 4 (over y, x), pipe: 2 (over core), tensor: 4 (over z).
Axes of the slice: x: 2, y: 2, z: 4, core: 2. Of those that a mesh axis runs over, the one named last changes fastest.
Arguments:
- inputs: bfloat16 [2, 896, 8192], P('pipe', 'dp', 'tensor'), may hold values from -6 to 6
- cotangent: bfloat16 [896, 8192], P('dp', 'tensor'), may hold values from -6 to 6
- up_first: bfloat16 [2, 32, 256, 256], P('pipe', 'tensor'), may hold values from -0.375 to 0.375
- up_second: bfloat16 [2, 32, 256, 1024], P('pipe', 'tensor'), may hold values from -0.375 to 0.375
- down_first: bfloat16 [2, 32, 1024, 256], P('pipe', 'tensor'), may hold values from -0.1875 to 0.1875
- down_second: bfloat16 [2, 32, 256, 256], P('pipe', 'tensor'), may hold values from -0.375 to 0.375
Outputs:
- grad_inputs: bfloat16 [2, 896, 8192], P('pipe', 'dp', 'tensor')
- grad_up_first: float32 [2, 32, 256, 256], P('pipe', 'tensor', 'dp')
- grad_up_second: float32 [2, 32, 256, 1024], P('pipe', 'tensor', 'dp')
- grad_down_first: float32 [2, 32, 1024, 256], P('pipe', 'tensor', 'dp')
- grad_down_second: float32 [2, 32, 256, 256], P('pipe', 'tensor', 'dp')
All inputs are finite; a program needn't handle non-finite values.
Results may differ from a plain program's by a relative error of at most 0.018.
Values may be sent and summed in bfloat16 or wider, within the bound.
A program may use at most 128 MiB of HBM per device.

v0:
```python
import math

import jax
import jax.numpy as jnp
from jax import lax
from jax.sharding import PartitionSpec as P

root_half = 1.0 / math.sqrt(2.0)
norm_density = 1.0 / math.sqrt(2.0 * math.pi)


def from_behind(value, axis, by):
    peers = lax.axis_size(axis)
    pairs = [(i, i + by) for i in range(peers) if 0 <= i + by < peers]
    return lax.ppermute(value, axis, pairs)


def gelu_value(values):
    return values * 0.5 * (1.0 + jax.scipy.special.erf(values * root_half))


def gelu_slope(values):
    cumulative = 0.5 * (1.0 + jax.scipy.special.erf(values * root_half))
    return cumulative + values * jnp.exp(-0.5 * values * values) * norm_density


def to_blocks(matrix, local_blocks):
    row_count = matrix.shape[0]
    return matrix.reshape(row_count, local_blocks, -1).transpose(1, 0, 2)


def from_blocks(blocked):
    return blocked.transpose(1, 0, 2).reshape(blocked.shape[1], -1)


def mix_layout(blocked, total_blocks):
    local_blocks, row_count, width = blocked.shape
    stride = width // total_blocks
    shaped = blocked.reshape(local_blocks, row_count, total_blocks, stride).transpose(2, 0, 3, 1)
    return shaped.reshape(total_blocks, local_blocks * stride, row_count)


def grad_path(incoming, slope_rows, weights, total_blocks):
    up_first, up_second, down_first, down_second = weights
    grad_blocks = to_blocks(incoming, up_first.shape[0])
    grad_last = jnp.einsum(
        "ite,ice->itc", grad_blocks, down_second, preferred_element_type=jnp.float32
    ).astype(jnp.bfloat16)
    grad_down = lax.all_to_all(
        mix_layout(grad_last, total_blocks), "tensor", split_axis=0, concat_axis=1, tiled=True
    )
    grad_hidden = jnp.einsum(
        "jct,jhc->jth", grad_down, down_first, preferred_element_type=jnp.float32
    )
    grad_pre = (grad_hidden * slope_rows).astype(jnp.bfloat16)
    grad_mixed = jnp.einsum(
        "jth,jch->jtc", grad_pre, up_second, preferred_element_type=jnp.float32
    ).astype(jnp.bfloat16)
    grad_first = lax.all_to_all(
        mix_layout(grad_mixed, total_blocks), "tensor", split_axis=0, concat_axis=1, tiled=True
    )
    grad_acts = jnp.einsum("iet,ice->itc", grad_first, up_first, preferred_element_type=jnp.float32)
    outgoing = (incoming.astype(jnp.float32) + from_blocks(grad_acts)).astype(jnp.bfloat16)
    return (outgoing, grad_down, grad_pre, grad_first)


def body(inputs, cotangent, up_first, up_second, down_first, down_second):
    weights = (up_first[0], up_second[0], down_first[0], down_second[0])
    local_blocks = up_first.shape[1]
    total_blocks = local_blocks * lax.axis_size("tensor")
    token_count = cotangent.shape[0]
    act_blocks = to_blocks(inputs[0], local_blocks)
    first = jnp.einsum(
        "itc,ice->ite", act_blocks, weights[0], preferred_element_type=jnp.float32
    ).astype(jnp.bfloat16)
    mixed = lax.all_to_all(
        mix_layout(first, total_blocks), "tensor", split_axis=0, concat_axis=1, tiled=True
    )
    pre_act = jnp.einsum("jct,jch->jth", mixed, weights[1], preferred_element_type=jnp.float32)
    hidden = gelu_value(pre_act).astype(jnp.bfloat16)
    slope = gelu_slope(pre_act)
    down = jnp.einsum(
        "jth,jhc->jtc", hidden, weights[2], preferred_element_type=jnp.float32
    ).astype(jnp.bfloat16)
    last = lax.all_to_all(
        mix_layout(down, total_blocks), "tensor", split_axis=0, concat_axis=1, tiled=True
    )
    section = lax.axis_index("pipe")
    sections = lax.axis_size("pipe")
    saved = (
        jnp.zeros_like(cotangent),
        jnp.zeros_like(mixed),
        jnp.zeros_like(hidden),
        jnp.zeros_like(mixed),
        jnp.zeros_like(cotangent),
    )
    current = cotangent
    for turn_index in range(sections):
        results = grad_path(current, slope, weights, total_blocks)
        taking = section == sections - 1 - turn_index
        fresh_parts = results + (current,)
        saved = tuple((jnp.where(taking, fresh, older) for fresh, older in zip(fresh_parts, saved)))
        if turn_index + 1 < sections:
            current = from_behind(results[0], "pipe", -1)
    grad_out, grad_down, grad_pre, grad_first, section_grad = saved
    factor = 1.0 / math.sqrt(token_count * lax.axis_size("dp"))
    grad_blocks = to_blocks(section_grad, local_blocks)
    term_first = (
        jnp.einsum("itc,iet->ice", act_blocks, grad_first, preferred_element_type=jnp.float32)
        * factor
    )
    term_second = (
        jnp.einsum("jct,jth->jch", mixed, grad_pre, preferred_element_type=jnp.float32) * factor
    )
    term_down = (
        jnp.einsum("jth,jct->jhc", hidden, grad_down, preferred_element_type=jnp.float32) * factor
    )
    term_last = (
        jnp.einsum("ict,ite->ice", last, grad_blocks, preferred_element_type=jnp.float32) * factor
    )
    reduced = (
        lax.psum_scatter(
            term_first.astype(jnp.bfloat16), "dp", scatter_dimension=1, tiled=True
        ).astype(jnp.float32),
        lax.psum_scatter(
            term_second.astype(jnp.bfloat16), "dp", scatter_dimension=1, tiled=True
        ).astype(jnp.float32),
        lax.psum_scatter(
            term_down.astype(jnp.bfloat16), "dp", scatter_dimension=1, tiled=True
        ).astype(jnp.float32),
        lax.psum_scatter(
            term_last.astype(jnp.bfloat16), "dp", scatter_dimension=1, tiled=True
        ).astype(jnp.float32),
    )
    return (grad_out[None], reduced[0][None], reduced[1][None], reduced[2][None], reduced[3][None])


def solution(mesh):
    return jax.shard_map(
        body,
        mesh=mesh,
        in_specs=(
            P("pipe", "dp", "tensor"),
            P("dp", "tensor"),
            P("pipe", "tensor", None, None),
            P("pipe", "tensor", None, None),
            P("pipe", "tensor", None, None),
            P("pipe", "tensor", None, None),
        ),
        out_specs=(
            P("pipe", "dp", "tensor"),
            P("pipe", "tensor", "dp", None),
            P("pipe", "tensor", "dp", None),
            P("pipe", "tensor", "dp", None),
            P("pipe", "tensor", "dp", None),
        ),
        check_vma=False,
    )
```

profile of v0, /device:TPU:0, one launch (start us, length us, event | category | flops | bytes accessed | tf_op | source)
XLA Modules:
  0.0 402.1 jit_solution(3821018633578911715)
XLA Ops:
  13.6 6.3 %all-to-all-start.1 = ((bf16[32,64,224]{2,1,0:T(8,128)(2,1)}), bf16[32,64,224]{2,1,0:T(8,128)(2,1)S(1)}, u32[]{:S(2)}, u32[]{:S(2)}) async-start(bf16[32,64,224]{2,1,0:T(8,128)(2,1)} %copy_bitcast_fusion.4), calls=%async_computation.1 | async-start | bytes 2097152 | tf_op jit(solution)/shard_map/all_to_all | solution.py:76
  19.9 2.6 convolution_convert_fusion.2
  27.1 18.5 %all-to-all-done.1 = bf16[32,64,224]{2,1,0:T(8,128)(2,1)S(1)} async-done(((bf16[32,64,224]{2,1,0:T(8,128)(2,1)}), bf16[32,64,224]{2,1,0:T(8,128)(2,1)S(1)}, u32[]{:S(2)}, u32[]{:S(2)}) %all-to-all-start.1) | async-done | bytes 917536 | tf_op jit(solution)/shard_map/all_to_all | solution.py:76
  45.6 4.2 %all-to-all-start = ((bf16[32,64,224]{2,1,0:T(8,128)(2,1)}), bf16[32,64,224]{2,1,0:T(8,128)(2,1)}, u32[]{:S(2)}, u32[]{:S(2)}) async-start(bf16[32,64,224]{2,1,0:T(8,128)(2,1)} %copy_bitcast_fusion.5), calls=%async_computation | async-start | bytes 2097152 | tf_op jit(solution)/shard_map/all_to_all | solution.py:49
  51.1 24.0 %all-to-all-done = bf16[32,64,224]{2,1,0:T(8,128)(2,1)} async-done(((bf16[32,64,224]{2,1,0:T(8,128)(2,1)}), bf16[32,64,224]{2,1,0:T(8,128)(2,1)}, u32[]{:S(2)}, u32[]{:S(2)}) %all-to-all-start) | async-done | bytes 917536 | tf_op jit(solution)/shard_map/all_to_all | solution.py:49
  76.4 5.3 %multiply_convert_fusion.2 = (bf16[8,224,1024]{2,1,0:T(8,128)(2,1)}, f32[8,224,1024]{2,1,0:T(8,128)S(1)}) fusion(bf16[8,256,224]{2,1,0:T(8,128)(2,1)S(1)} %bitcast.171, bf16[1,8,256,1024]{3,2,1,0:T(8,128)(2,1)} %param.9), kind=kOutput, calls=%fused_computation.7 | convolution fusion | flops 948699136 | bytes 16121856 | tf_op jit(solution)/shard_map/jct,jch->jth/dot_general | solution.py:79
  81.8 4.0 multiply_convert_fusion.4
  93.5 27.7 %all_to_all.108 = bf16[32,64,224]{2,1,0:T(8,128)(2,1)S(1)} all-to-all(bf16[32,64,224]{2,1,0:T(8,128)(2,1)S(1)} %copy_bitcast_fusion.3), channel_id=1, replica_groups=mesh['dp'=4,'pipe'=2,'tensor'=4] {'tensor'}, dimensions={0} | all-to-all | bytes 1835008 | tf_op jit(solution)/shard_map/all_to_all | solution.py:59
  125.5 3.1 collective-permute-done
  134.7 28.9 %all_to_all.109 = bf16[32,64,224]{2,1,0:T(8,128)(2,1)S(1)} all-to-all(bf16[32,64,224]{2,1,0:T(8,128)(2,1)S(1)} %copy_bitcast_fusion.2), channel_id=1, replica_groups=mesh['dp'=4,'pipe'=2,'tensor'=4] {'tensor'}, dimensions={0} | all-to-all | bytes 1835008 | tf_op jit(solution)/shard_map/all_to_all | solution.py:49
  163.7 6.5 %multiply_convert_fusion.3 = bf16[8,224,1024]{2,1,0:T(8,128)(2,1)S(1)} fusion(bf16[8,256,224]{2,1,0:T(8,128)(2,1)S(1)} %bitcast.185, bf16[1,8,1024,256]{3,2,1,0:T(8,128)(2,1)S(1)} %copy-done.19, f32[8,224,1024]{2,1,0:T(8,128)} %copy-done.2), kind=kOutput, calls=%fused_computation.8 | convolution fusion | flops 957874176 | bytes 16121856 | tf_op jit(solution)/shard_map/jct,jhc->jth/dot_general | solution.py:52
  178.9 4.3 %all-to-all-start.4 = ((bf16[32,64,224]{2,1,0:T(8,128)(2,1)}), bf16[32,64,224]{2,1,0:T(8,128)(2,1)}, u32[]{:S(2)}, u32[]{:S(2)}) async-start(bf16[32,64,224]{2,1,0:T(8,128)(2,1)} %copy_bitcast_fusion.1), calls=%async_computation.4 | async-start | bytes 2097152 | tf_op jit(solution)/shard_map/all_to_all | solution.py:59
  183.2 5.3 %fusion.28 = bf16[8,224,256]{2,1,0:T(8,128)(2,1)} fusion(bf16[8,224,1024]{2,1,0:T(8,128)(2,1)} %get-tuple-element.22, bf16[1,8,1024,256]{3,2,1,0:T(8,128)(2,1)} %param.10), kind=kOutput, calls=%fused_computation.35 | convolution fusion | flops 939982848 | bytes 8781824 | tf_op jit(solution)/shard_map/jth,jhc->jtc/dot_general | solution.py:82
  193.1 15.6 %all-to-all-done.4 = bf16[32,64,224]{2,1,0:T(8,128)(2,1)} async-done(((bf16[32,64,224]{2,1,0:T(8,128)(2,1)}), bf16[32,64,224]{2,1,0:T(8,128)(2,1)}, u32[]{:S(2)}, u32[]{:S(2)}) %all-to-all-start.4) | async-done | bytes 917536 | tf_op jit(solution)/shard_map/all_to_all | solution.py:59
  208.7 4.2 %all-to-all-start.5 = ((bf16[32,64,224]{2,1,0:T(8,128)(2,1)}), bf16[32,64,224]{2,1,0:T(8,128)(2,1)}, u32[]{:S(2)}, u32[]{:S(2)}) async-start(bf16[32,64,224]{2,1,0:T(8,128)(2,1)} %copy_bitcast_fusion), calls=%async_computation.8 | async-start | bytes 2097152 | tf_op jit(solution)/shard_map/all_to_all | solution.py:85
  215.4 2.6 fusion.37
  220.8 17.4 %all-to-all-done.5 = bf16[32,64,224]{2,1,0:T(8,128)(2,1)} async-done(((bf16[32,64,224]{2,1,0:T(8,128)(2,1)}), bf16[32,64,224]{2,1,0:T(8,128)(2,1)}, u32[]{:S(2)}, u32[]{:S(2)}) %all-to-all-start.5) | async-done | bytes 917536 | tf_op jit(solution)/shard_map/all_to_all | solution.py:85
  244.3 5.3 %multiply_convert_fusion.1 = bf16[8,256,1024]{2,1,0:T(8,128)(2,1)} fusion(bf16[8,256,224]{2,1,0:T(8,128)(2,1)S(1)} %bitcast.172, bf16[8,224,1024]{2,1,0:T(8,128)(2,1)} %copy-done.21, bf16[8,224,1024]{2,1,0:T(8,128)(2,1)} %copy-done.20, pred[]{:T(512)S(6)} %eq.7, pred[]{:T(512)S(6)} %eq.6), kind=kOutput, calls=%fused_computation.2 | convolution fusion | flops 947388416 | bytes 12451842 | tf_op jit(solution)/shard_map/jct,jth->jch/dot_general | solution.py:113
  251.2 5.7 %multiply_convert_fusion = bf16[8,1024,256]{2,1,0:T(8,128)(2,1)} fusion(bf16[8,224,1024]{2,1,0:T(8,128)(2,1)} %get-tuple-element.22, bf16[8,256,224]{2,1,0:T(8,128)(2,1)S(1)} %bitcast.186, bf16[8,256,224]{2,1,0:T(8,128)(2,1)S(1)} %bitcast.184, pred[]{:T(512)S(6)} %eq.7, pred[]{:T(512)S(6)} %eq.6), kind=kOutput, calls=%fused_computation.1 | convolution fusion | flops 944635904 | bytes 9699330 | tf_op jit(solution)/shard_map/jth,jct->jhc/dot_general | solution.py:116
  258.9 22.4 %reduce-scatter.11.cloned.1.call-done = bf16[8,64,256]{2,1,0:T(8,128)(2,1)} async-done(((bf16[8,256,256]{2,1,0:T(8,128)(2,1)}), bf16[8,64,256]{2,1,0:T(8,128)(2,1)}) %reduce-scatter.11.cloned.1.call-update) | async-done | bytes 262160 | tf_op jit(solution)/shard_map/reduce_scatter | solution.py:131
  283.1 53.9 %reduce-scatter.7.cloned.1.call-done = bf16[8,64,1024]{2,1,0:T(8,128)(2,1)} async-done(((bf16[8,256,1024]{2,1,0:T(8,128)(2,1)}), bf16[8,64,1024]{2,1,0:T(8,128)(2,1)}) %reduce-scatter.7.cloned.1.call-update) | async-done | bytes 1048592 | tf_op jit(solution)/shard_map/reduce_scatter | solution.py:125
  337.0 2.8 bitcast_convert_fusion.1
  339.7 53.0 %reduce-scatter.9.cloned.1.call-done = bf16[8,256,256]{2,1,0:T(8,128)(2,1)} async-done(((bf16[8,1024,256]{2,1,0:T(8,128)(2,1)}), bf16[8,256,256]{2,1,0:T(8,128)(2,1)}) %reduce-scatter.9.cloned.1.call-update) | async-done | bytes 1048592 | tf_op jit(solution)/shard_map/reduce_scatter | solution.py:128
  392.8 2.7 bitcast_convert_fusion
  (88 shorter events, 61.5 us)
Async XLA Ops:
  7.2 2.5 copy-start
  9.6 10.2 %copy-start.1 = (bf16[224,2048]{1,0:T(8,128)(2,1)S(1)}, bf16[224,2048]{1,0:T(8,128)(2,1)}, u32[]{:S(2)}) copy-start(bf16[224,2048]{1,0:T(8,128)(2,1)} %param.7) | copy-start | bytes 2752516
  13.6 32.0 %all-to-all-start.1 = ((bf16[32,64,224]{2,1,0:T(8,128)(2,1)}), bf16[32,64,224]{2,1,0:T(8,128)(2,1)S(1)}, u32[]{:S(2)}, u32[]{:S(2)}) async-start(bf16[32,64,224]{2,1,0:T(8,128)(2,1)} %copy_bitcast_fusion.4), calls=%async_computation.1 | async-start | bytes 2097152 | tf_op jit(solution)/shard_map/all_to_all | solution.py:76
  45.6 4.2 %copy-start.3 = (bf16[32,64,224]{2,1,0:T(8,128)(2,1)}, bf16[32,64,224]{2,1,0:T(8,128)(2,1)S(1)}, u32[]{:S(2)}) copy-start(bf16[32,64,224]{2,1,0:T(8,128)(2,1)S(1)} %all-to-all-done.1) | copy-start | bytes 2752516
  45.6 29.5 %all-to-all-start = ((bf16[32,64,224]{2,1,0:T(8,128)(2,1)}), bf16[32,64,224]{2,1,0:T(8,128)(2,1)}, u32[]{:S(2)}, u32[]{:S(2)}) async-start(bf16[32,64,224]{2,1,0:T(8,128)(2,1)} %copy_bitcast_fusion.5), calls=%async_computation | async-start | bytes 2097152 | tf_op jit(solution)/shard_map/all_to_all | solution.py:49
  76.4 5.4 %copy-start.14 = (bf16[8,4,64,224]{3,2,1,0:T(8,128)(2,1)}, bf16[8,4,64,224]{3,2,1,0:T(8,128)(2,1)S(1)}, u32[]{:S(2)}) copy-start(bf16[8,4,64,224]{3,2,1,0:T(8,128)(2,1)S(1)} %copy.52) | copy-start | bytes 2752516
  76.4 5.4 %copy-start.18 = (bf16[1,8,1024,256]{3,2,1,0:T(8,128)(2,1)S(1)}, bf16[1,8,1024,256]{3,2,1,0:T(8,128)(2,1)}, u32[]{:S(2)}) copy-start(bf16[1,8,1024,256]{3,2,1,0:T(8,128)(2,1)} %param.10) | copy-start | bytes 12582916
  81.8 4.0 copy-start.2
  81.8 5.8 %copy-start.6 = (bf16[1,8,256,1024]{3,2,1,0:T(8,128)(2,1)S(1)}, bf16[1,8,256,1024]{3,2,1,0:T(8,128)(2,1)}, u32[]{:S(2)}) copy-start(bf16[1,8,256,1024]{3,2,1,0:T(8,128)(2,1)} %param.9) | copy-start | bytes 12582916
  85.8 1.8 copy-start.20
  122.8 6.8 %copy-start.8 = (bf16[1,8,256,256]{3,2,1,0:T(8,128)(2,1)S(1)}, bf16[1,8,256,256]{3,2,1,0:T(8,128)(2,1)}, u32[]{:S(2)}) copy-start(bf16[1,8,256,256]{3,2,1,0:T(8,128)(2,1)} %param.11) | copy-start | bytes 3145732
  124.2 4.4 %collective-permute-start = (bf16[224,2048]{1,0:T(8,128)(2,1)S(1)}, bf16[224,2048]{1,0:T(8,128)(2,1)S(1)}, u32[]{:S(2)}, u32[]{:S(2)}) collective-permute-start(bf16[224,2048]{1,0:T(8,128)(2,1)S(1)} %add_convert_fusion.1), channel_id=1, source_target_pairs={{4,0},{5,1},{6,2},{7,3},{12,8},{13,9},{14,10},{15,11},{20,16},{21,... | collective-permute-start | bytes 2752520 | tf_op jit(solution)/shard_map/ppermute | solution.py:15
  133.2 30.5 %copy-start.19 = (bf16[1,8,1024,256]{3,2,1,0:T(8,128)(2,1)S(1)}, bf16[1,8,1024,256]{3,2,1,0:T(8,128)(2,1)}, u32[]{:S(2)}) copy-start(bf16[1,8,1024,256]{3,2,1,0:T(8,128)(2,1)} %param.10) | copy-start | bytes 12582916
  163.6 6.5 %copy-start.16 = (bf16[8,4,64,224]{3,2,1,0:T(8,128)(2,1)}, bf16[8,4,64,224]{3,2,1,0:T(8,128)(2,1)S(1)}, u32[]{:S(2)}) copy-start(bf16[8,4,64,224]{3,2,1,0:T(8,128)(2,1)S(1)} %copy.67) | copy-start | bytes 2752516
  163.7 8.3 %copy-start.7 = (bf16[1,8,256,1024]{3,2,1,0:T(8,128)(2,1)S(1)}, bf16[1,8,256,1024]{3,2,1,0:T(8,128)(2,1)}, u32[]{:S(2)}) copy-start(bf16[1,8,256,1024]{3,2,1,0:T(8,128)(2,1)} %param.9) | copy-start | bytes 12582916
  170.2 1.8 copy-start.21
  178.9 29.7 %all-to-all-start.4 = ((bf16[32,64,224]{2,1,0:T(8,128)(2,1)}), bf16[32,64,224]{2,1,0:T(8,128)(2,1)}, u32[]{:S(2)}, u32[]{:S(2)}) async-start(bf16[32,64,224]{2,1,0:T(8,128)(2,1)} %copy_bitcast_fusion.1), calls=%async_computation.4 | async-start | bytes 2097152 | tf_op jit(solution)/shard_map/all_to_all | solution.py:59
  208.7 29.5 %all-to-all-start.5 = ((bf16[32,64,224]{2,1,0:T(8,128)(2,1)}), bf16[32,64,224]{2,1,0:T(8,128)(2,1)}, u32[]{:S(2)}, u32[]{:S(2)}) async-start(bf16[32,64,224]{2,1,0:T(8,128)(2,1)} %copy_bitcast_fusion), calls=%async_computation.8 | async-start | bytes 2097152 | tf_op jit(solution)/shard_map/all_to_all | solution.py:85
  212.9 44.1 %reduce-scatter.5.cloned.1.call-start = ((), (), s32[]{:S(2)}) async-start(), calls=%async_computation.10 | async-start | bytes 1310720 | tf_op jit(solution)/shard_map/reduce_scatter | solution.py:122
  220.7 60.6 %reduce-scatter.11.cloned.1.call-start = ((), (), s32[]{:S(2)}) async-start(), calls=%async_computation.13 | async-start | bytes 1310720 | tf_op jit(solution)/shard_map/reduce_scatter | solution.py:131
  239.5 2.1 copy-start.11
  239.5 2.1 copy-start.13
  244.3 92.7 %reduce-scatter.7.cloned.1.call-start = ((), (), s32[]{:S(2)}) async-start(), calls=%async_computation.11 | async-start | bytes 5242880 | tf_op jit(solution)/shard_map/reduce_scatter | solution.py:125
  249.7 143.1 %reduce-scatter.9.cloned.1.call-start = ((), (), s32[]{:S(2)}) async-start(), calls=%async_computation.12 | async-start | bytes 5242880 | tf_op jit(solution)/shard_map/reduce_scatter | solution.py:128
  (7 other events, 7.5 us)
Sparse Core Ops, SparseCore 0:
  220.8 28.8 reduce-scatter.4
  253.5 27.7 reduce-scatter.10
  284.2 52.6 reduce-scatter.6
  340.0 52.6 reduce-scatter.8
where the time goes:
time: 403 us; the launch traced here: 402 us
  waiting for transfers between devices  208 us (52%)
  blocking collectives  56.5 us (14%)
  matrix products  48.6 us (12%)
  local copies, waits for them, and re-layouts  44.3 us (11%)
  starting transfers between devices  20.7 us (5%)
  between operations  14.1 us (3%)
  other arithmetic  9.78 us (2%)
    reduce_scatter x1, waiting for transfers between devices, body(): lax.psum_scatter(term_second.astype(jnp.bfloat16), 'dp', scatter_dimensio...  53.9 us
    reduce_scatter x1, waiting for transfers between devices, body(): lax.psum_scatter(term_down.astype(jnp.bfloat16), 'dp', scatter_dimension=...  53 us
    all_to_all x1, blocking collectives, grad_path(): lax.all_to_all(mix_layout(grad_last, total_blocks), 'tensor', split_axis=...  28.9 us
    all_to_all x1, blocking collectives, grad_path(): lax.all_to_all(mix_layout(grad_mixed, total_blocks), 'tensor', split_axis...  27.7 us
    all_to_all x1, waiting for transfers between devices, grad_path(): lax.all_to_all(mix_layout(grad_last, total_blocks), 'tensor', split_axis=...  24 us
    reduce_scatter x1, waiting for transfers between devices, body(): lax.psum_scatter(term_last.astype(jnp.bfloat16), 'dp', scatter_dimension=...  22.4 us
    all_to_all x1, waiting for transfers between devices, body(): lax.all_to_all(mix_layout(first, total_blocks), 'tensor', split_axis=0, c...  18.5 us
    all_to_all x1, waiting for transfers between devices, body(): lax.all_to_all(mix_layout(down, total_blocks), 'tensor', split_axis=0, co...  17.4 us
  transfers between devices with their start and end apart: 9, of which 8 were waited for; matrix products, arithmetic and copies ran while one was open for 12% of the time, Pallas kernels for 0%

commit v1 on v0

v1 whole, which is shorter than its diff:
```python
import math

import jax
import jax.numpy as jnp
from jax import lax
from jax.experimental import pallas as pl
from jax.experimental.pallas import tpu as pltpu
from jax.sharding import PartitionSpec as P

MESH = pl.DeviceIdType.MESH
root_half = 1.0 / math.sqrt(2.0)
norm_density = 1.0 / math.sqrt(2.0 * math.pi)
lanes = 128
f32 = jnp.float32
bf16 = jnp.bfloat16


def mm(left, right, left_dim, right_dim):
    return lax.dot_general(
        left, right, (((left_dim,), (right_dim,)), ((), ())), preferred_element_type=f32
    )


def make_kernel(sizes, factor):
    nt, nd, ns, lb, bs, hb, tp = sizes
    stride = bs // (nt * lb)
    rows = lb * stride

    def kernel(
        x_ref, cot_ref, w1, w2, w3, w4,
        gout, r1, r2, r3, r4,
        gbuf, sbuf, rbuf, hidden, slope, gpre, st1, st2, st3, st4,
        a_send, a_recv, d_send, d_recv, own_sem, p_send, p_recv,
    ):
        me_t = lax.axis_index("tensor")
        me_d = lax.axis_index("dp")
        me_s = lax.axis_index("pipe")
        is_last = me_s == ns - 1
        not_last = me_s < ns - 1
        not_first = me_s > 0

        barrier = pltpu.get_barrier_semaphore()
        for k in range(1, nt):
            pl.semaphore_signal(
                barrier, inc=1, device_id={"tensor": lax.rem(me_t + k, nt)}, device_id_type=MESH
            )
        for k in range(1, nd):
            pl.semaphore_signal(
                barrier, inc=1, device_id={"dp": lax.rem(me_d + k, nd)}, device_id_type=MESH
            )

        for k in range(1, ns):
            pl.semaphore_signal(
                barrier, inc=1, device_id={"pipe": lax.rem(me_s + k, ns)}, device_id_type=MESH
            )
        pl.semaphore_wait(barrier, nt - 1 + nd - 1 + ns - 1)

        def cols(i):
            return pl.ds(pl.multiple_of(i * bs, bs), bs)

        def produce(which, make):
            def pair(p, carry):
                parts = [make(2 * p + u).reshape(nt, lb, stride, tp) for u in range(2)]
                both = jnp.concatenate(parts, axis=2).astype(bf16)
                at = pl.multiple_of(p * 2 * stride, 2 * stride)
                sbuf[which, :, :, pl.ds(at, 2 * stride), :] = both
                return carry

            lax.fori_loop(0, lb // 2, pair, 0)

        def a2a(which, k):
            peer = lax.rem(me_t + k, nt)
            return pltpu.make_async_remote_copy(
                src_ref=sbuf.at[which, peer],
                dst_ref=rbuf.at[which, me_t],
                send_sem=a_send.at[which, k],
                recv_sem=a_recv.at[which, k],
                device_id={"tensor": peer},
                device_id_type=MESH,
            )

        def send(which):
            for k in range(1, nt):
                a2a(which, k).start()
            rbuf[which, me_t] = sbuf[which, me_t]

        def arrive(which):
            for k in range(1, nt):
                a2a(which, k).wait_recv()

        def block(which, j):
            return rbuf[which, :, j].reshape(bs, tp)

        pairs = ((st1, r1), (st2, r2), (st3, r3), (st4, r4))

        def share(which, k):
            staged, landed = pairs[which]
            peer = lax.rem(me_d + k, nd)
            return pltpu.make_async_remote_copy(
                src_ref=staged.at[peer],
                dst_ref=landed.at[me_d],
                send_sem=d_send.at[which, k],
                recv_sem=d_recv.at[which, k],
                device_id={"dp": peer},
                device_id_type=MESH,
            )

        def own(which):
            staged, landed = pairs[which]
            return pltpu.make_async_copy(staged.at[me_d], landed.at[me_d], own_sem.at[which])

        def spread(which):
            for k in range(1, nd):
                share(which, k).start()
            own(which).start()

        def hand_on():
            return pltpu.make_async_remote_copy(
                src_ref=gout,
                dst_ref=gbuf,
                send_sem=p_send,
                recv_sem=p_recv,
                device_id={"pipe": lax.rem(me_s + ns - 1, ns)},
                device_id_type=MESH,
            )

        def make_first(i):
            return mm(w1[i], x_ref[:, cols(i)], 0, 1)

        def make_grad_last(i):
            return mm(w4[i], gbuf[:, cols(i)], 1, 1)

        def make_down(j):
            return mm(w3[j], hidden[j], 0, 0)

        def make_grad_mixed(j):
            grad_hidden = mm(w3[j], block(1, j), 1, 0)
            grad_pre = (grad_hidden * slope[j]).astype(bf16)
            gpre[j] = grad_pre
            return mm(w2[j], grad_pre, 1, 0)

        @pl.when(is_last)
        def _():
            gbuf[...] = cot_ref[...]
            produce(1, make_grad_last)
            send(1)

        produce(0, make_first)
        send(0)
        arrive(0)

        def forward(j, carry):
            pre = mm(w2[j], block(0, j), 0, 0)
            cumulative = 0.5 * (1.0 + lax.erf(pre * root_half))
            hidden[j] = (pre * cumulative).astype(bf16)
            slope[j] = cumulative + pre * jnp.exp(-0.5 * pre * pre) * norm_density
            return carry

        lax.fori_loop(0, lb, forward, 0)

        @pl.when(not_last)
        def _():
            produce(2, make_down)
            send(2)
            hand_on().wait_recv()
            produce(1, make_grad_last)
            send(1)

        arrive(1)
        produce(3, make_grad_mixed)
        send(3)

        @pl.when(is_last)
        def _():
            produce(2, make_down)
            send(2)

        def grad_second(j, carry):
            value = mm(block(0, j), gpre[j], 1, 1) * factor
            st2[:, j] = value.astype(bf16).reshape(nd, bs // nd, hb)
            return carry

        def grad_down(j, carry):
            value = mm(hidden[j], block(1, j), 1, 1) * factor
            st3[:, j] = value.astype(bf16).reshape(nd, hb // nd, bs)
            return carry

        lax.fori_loop(0, lb, grad_second, 0)
        spread(1)
        lax.fori_loop(0, lb, grad_down, 0)
        spread(2)

        arrive(3)

        def outgoing(i, carry):
            acts = mm(w1[i], block(3, i), 1, 0).T
            gout[:, cols(i)] = (gbuf[:, cols(i)].astype(f32) + acts).astype(bf16)
            return carry

        lax.fori_loop(0, lb, outgoing, 0)

        @pl.when(not_first)
        def _():
            hand_on().start()

        def grad_first(i, carry):
            value = mm(x_ref[:, cols(i)].T, block(3, i), 1, 1) * factor
            st1[:, i] = value.astype(bf16).reshape(nd, bs // nd, bs)
            return carry

        lax.fori_loop(0, lb, grad_first, 0)
        spread(0)
        arrive(2)

        def grad_last(i, carry):
            value = mm(block(2, i), gbuf[:, cols(i)], 1, 0) * factor
            st4[:, i] = value.astype(bf16).reshape(nd, bs // nd, bs)
            return carry

        lax.fori_loop(0, lb, grad_last, 0)
        spread(3)

        for which in range(4):
            for k in range(1, nt):
                a2a(which, k).wait_send()
        for which in range(4):
            own(which).wait()
            for k in range(1, nd):
                share(which, k).wait()

        @pl.when(not_first)
        def _():
            hand_on().wait_send()

    return kernel


def body(inputs, cotangent, up_first, up_second, down_first, down_second):
    nt, nd, ns = (lax.axis_size(a) for a in ("tensor", "dp", "pipe"))
    tokens, width = cotangent.shape
    lb, bs, hb = up_second.shape[1:]
    tp = -(-tokens // lanes) * lanes
    factor = 1.0 / math.sqrt(tokens * nd)
    pad = ((0, tp - tokens), (0, 0))
    vmem = pl.BlockSpec(memory_space=pltpu.VMEM)
    anywhere = pl.BlockSpec(memory_space=pl.ANY)
    shapes = (
        (nd, lb, bs // nd, bs),
        (nd, lb, bs // nd, hb),
        (nd, lb, hb // nd, bs),
        (nd, lb, bs // nd, bs),
    )
    stride = bs // (nt * lb)
    exchange = (4, nt, lb, lb * stride, tp)
    dma = pltpu.SemaphoreType.DMA
    flops = 2 * tp * lb * bs * (8 * bs + 10 * hb)
    out = pl.pallas_call(
        make_kernel((nt, nd, ns, lb, bs, hb, tp), factor),
        out_shape=(jax.ShapeDtypeStruct((tp, width), bf16),)
        + tuple(jax.ShapeDtypeStruct(s, bf16) for s in shapes),
        in_specs=[vmem] * 6,
        out_specs=(vmem,) + (anywhere,) * 4,
        scratch_shapes=[
            pltpu.VMEM((tp, width), bf16),
            pltpu.VMEM(exchange, bf16),
            pltpu.VMEM(exchange, bf16),
            pltpu.VMEM((lb, hb, tp), bf16),
            pltpu.VMEM((lb, hb, tp), f32),
            pltpu.VMEM((lb, hb, tp), bf16),
        ]
        + [pltpu.VMEM(s, bf16) for s in shapes]
        + [
            dma((4, nt)),
            dma((4, nt)),
            dma((4, nd)),
            dma((4, nd)),
            dma((4,)),
            dma,
            dma,
        ],
        compiler_params=pltpu.CompilerParams(
            collective_id=0, has_side_effects=True, vmem_limit_bytes=60 * 1024 * 1024
        ),
        cost_estimate=pl.CostEstimate(
            flops=flops, bytes_accessed=8 * lb * bs * hb, transcendentals=2 * lb * hb * tp
        ),
    )(
        jnp.pad(inputs[0], pad),
        jnp.pad(cotangent, pad),
        up_first[0],
        up_second[0],
        down_first[0],
        down_second[0],
    )
    sums = tuple(jnp.sum(part.astype(f32), axis=0)[None] for part in out[1:])
    return (out[0][None, :tokens],) + sums


def solution(mesh):
    return jax.shard_map(
        body,
        mesh=mesh,
        in_specs=(
            P("pipe", "dp", "tensor"),
            P("dp", "tensor"),
            P("pipe", "tensor", None, None),
            P("pipe", "tensor", None, None),
            P("pipe", "tensor", None, None),
            P("pipe", "tensor", None, None),
        ),
        out_specs=(
            P("pipe", "dp", "tensor"),
            P("pipe", "tensor", "dp", None),
            P("pipe", "tensor", "dp", None),
            P("pipe", "tensor", "dp", None),
            P("pipe", "tensor", "dp", None),
        ),
        check_vma=False,
    )
```

time: 403 us -> 194 us (0.48)
  waiting for transfers between devices: 208 us -> 0 us
  Pallas kernels: 0 us -> 175 us
  blocking collectives: 56.5 us -> 0 us
  matrix products: 48.6 us -> 0 us
  local copies, waits for them, and re-layouts: 44.3 us -> 6.91 us
  starting transfers between devices: 20.7 us -> 0 us
  between operations: 14.1 us -> 0.65 us
    pallas_call x0 -> x1, Pallas kernels: none -> 175 us  [body(): pl.pallas_call(make_kernel((nt, nd, ns, lb, bs, hb, tp), factor), out_sha...]
    reduce_scatter x4 -> x0, waiting for transfers between devices: 129 us -> none  [the longest x1 53.9 us: body(): lax.psum_scatter(term_second.astype(jnp.bfloat16), 'dp', scatter_dimensio...]
    all_to_all x4 -> x0, waiting for transfers between devices: 75.5 us -> none  [the longest x1 24 us: grad_path(): lax.all_to_all(mix_layout(grad_last, total_blocks), 'tensor', split_axis=...]
    all_to_all x2 -> x0, blocking collectives: 56.5 us -> none  [the longest x1 28.9 us: grad_path(): lax.all_to_all(mix_layout(grad_last, total_blocks), 'tensor', split_axis=...]
    dot_general x15 -> x0, matrix products: 48.6 us -> none  [the longest x2 10.5 us: grad_path(): jnp.einsum('jct,jhc->jth', grad_down, down_first, preferred_element_type=...]
    all_to_all x4 -> x0, starting transfers between devices: 19 us -> none  [the longest x1 6.32 us: body(): lax.all_to_all(mix_layout(first, total_blocks), 'tensor', split_axis=0, c...]
    convert_element_type x7 -> x0, local copies, waits for them, and re-layouts: 15.3 us -> none  [the longest x2 4.47 us: grad_path(): grad_mixed = jnp.einsum('jth,jch->jtc', grad_pre, up_second, preferred_el...]
    unnamed x46 -> x4, local copies, waits for them, and re-layouts: 12.3 us -> 0.01 us
  transfers between devices with their start and end apart: 9 -> 0, of which waited for: 8 -> 0; matrix products, arithmetic and copies ran while one was open for 12% -> 0% of each run, Pallas kernels for 0% -> 0%
where the time goes in v1:
time: 194 us; the launch traced here: 190 us
  Pallas kernels  175 us (90%)
  other arithmetic  7.43 us (4%)
  local copies, waits for them, and re-layouts  6.91 us (4%)
    pallas_call x1, Pallas kernels, body(): pl.pallas_call(make_kernel((nt, nd, ns, lb, bs, hb, tp), factor), out_sha...  175 us
    reduce_sum x3, other arithmetic, body(): sums = tuple((jnp.sum(part.astype(f32), axis=0)[None] for part in out[1:]))  7.43 us

profile of v1, /device:TPU:0, one launch (start us, length us, event | category | flops | bytes accessed | tf_op | source)
XLA Modules:
  0.0 189.8 jit_solution(17615682036434554858)
XLA Ops:
  0.6 2.3 %pad.7.x_ref = bf16[256,2048]{1,0:T(8,128)(2,1)} pad(bf16[224,2048]{1,0:T(8,128)(2,1)} %bitcast.13, bf16[]{:T(256)} %constant.1.clone.1), padding=0_32x0_0 | pad | bytes 1966082 | tf_op jit(solution)/shard_map/jit(_pad)/pad | solution.py:288
  2.9 2.3 %pad.8.cot_ref = bf16[256,2048]{1,0:T(8,128)(2,1)} pad(bf16[224,2048]{1,0:T(8,128)(2,1)} %param.7, bf16[]{:T(256)} %constant.1.clone.1), padding=0_32x0_0 | pad | bytes 1966082 | tf_op jit(solution)/shard_map/jit(_pad)/pad | solution.py:289
  5.2 174.8 %shard_map.101 = (bf16[256,2048]{1,0:T(8,128)(2,1)}, bf16[4,8,64,256]{3,2,1,0:T(8,128)(2,1)}, bf16[4,8,64,1024]{3,2,1,0:T(8,128)(2,1)}, bf16[4,8,256,256]{3,2,1,0:T(8,128)(2,1)}, bf16[4,8,64,256]{3,2,1,0:T(8,128)(2,1)}) custom-call(bf16[256,2048]{1,0:T(8,128)(2,1)} %pad.7.x_ref, bf16[256,2048]{1,0:T(8,128)(2,1)} %pad.8.cot_ref, ...), custom_call_target="tpu_custom_call" | custom-call | flops 12884901888 | bytes 16777216 | tf_op jit(solution)/shard_map/pallas_call | solution.py:257
  180.0 0.0 copy-start.1
  180.0 2.3 %slice_bitcast_fusion = bf16[1,224,2048]{2,1,0:T(8,128)(2,1)} fusion(bf16[256,2048]{1,0:T(8,128)(2,1)} %get-tuple-element.10), kind=kLoop, calls=%fused_computation.4 | loop fusion | bytes 1835008 | tf_op jit(solution)/shard_map/broadcast_in_dim | solution.py:296
  182.3 0.0 copy-start
  182.3 3.2 %convert_reduce_fusion.2 = (f32[8,64,256]{2,1,0:T(8,128)}, f32[8,64,256]{2,1,0:T(8,128)}) fusion(bf16[4,8,64,256]{3,2,1,0:T(8,128)(2,1)} %get-tuple-element.14, bf16[4,8,64,256]{3,2,1,0:T(8,128)(2,1)} %get-tuple-element.11), kind=kLoop, calls=%fused_computation.2 | loop fusion | flops 1835008 | bytes 3145728 | tf_op jit(solution)/shard_map/reduce_sum | solution.py:295
  185.5 0.0 copy-done.1
  185.5 2.3 %convert_reduce_fusion.1 = f32[8,64,1024]{2,1,0:T(8,128)} fusion(bf16[4,8,64,1024]{3,2,1,0:T(8,128)(2,1)S(1)} %copy-done.1), kind=kLoop, calls=%fused_computation.1 | loop fusion | flops 3670016 | bytes 6291456 | tf_op jit(solution)/shard_map/reduce_sum | solution.py:295
  187.8 0.0 copy-done
  187.8 2.0 %convert_reduce_fusion = f32[8,256,256]{2,1,0:T(8,128)} fusion(bf16[4,8,256,256]{3,2,1,0:T(8,128)(2,1)S(1)} %copy-done), kind=kLoop, calls=%fused_computation | loop fusion | flops 3670016 | bytes 6291456 | tf_op jit(solution)/shard_map/reduce_sum | solution.py:295
Async XLA Ops:
  180.0 5.5 %copy-start.1 = (bf16[4,8,64,1024]{3,2,1,0:T(8,128)(2,1)S(1)}, bf16[4,8,64,1024]{3,2,1,0:T(8,128)(2,1)}, u32[]{:S(2)}) copy-start(bf16[4,8,64,1024]{3,2,1,0:T(8,128)(2,1)} %get-tuple-element.12) | copy-start | bytes 12582916
  182.3 5.4 %copy-start = (bf16[4,8,256,256]{3,2,1,0:T(8,128)(2,1)S(1)}, bf16[4,8,256,256]{3,2,1,0:T(8,128)(2,1)}, u32[]{:S(2)}) copy-start(bf16[4,8,256,256]{3,2,1,0:T(8,128)(2,1)} %get-tuple-element.13) | copy-start | bytes 12582916

commit v2 on v1

--- a/solution.py
+++ b/solution.py
@@ -21,7 +21,7 @@
     )
 
 
-def make_kernel(sizes, factor):
+def make_token_kernel(sizes, factor):
     nt, nd, ns, lb, bs, hb, tp = sizes
     stride = bs // (nt * lb)
     rows = lb * stride
@@ -235,7 +235,7 @@
     return kernel
 
 
-def body(inputs, cotangent, up_first, up_second, down_first, down_second):
+def tokens_split(inputs, cotangent, up_first, up_second, down_first, down_second):
     nt, nd, ns = (lax.axis_size(a) for a in ("tensor", "dp", "pipe"))
     tokens, width = cotangent.shape
     lb, bs, hb = up_second.shape[1:]
@@ -255,7 +255,7 @@
     dma = pltpu.SemaphoreType.DMA
     flops = 2 * tp * lb * bs * (8 * bs + 10 * hb)
     out = pl.pallas_call(
-        make_kernel((nt, nd, ns, lb, bs, hb, tp), factor),
+        make_token_kernel((nt, nd, ns, lb, bs, hb, tp), factor),
         out_shape=(jax.ShapeDtypeStruct((tp, width), bf16),)
         + tuple(jax.ShapeDtypeStruct(s, bf16) for s in shapes),
         in_specs=[vmem] * 6,
@@ -296,6 +296,344 @@
     return (out[0][None, :tokens],) + sums
 
 
+def make_block_kernel(sizes, factor):
+    nt, nd, ns, nb, bs, hb, tokens = sizes
+    group = nt * nd
+    stride = bs // (group * nb)
+    rows = nb * stride
+    total = nd * tokens
+    wide = nb * bs
+    pieces = hb // bs
+
+    def kernel(
+        x_hbm, cot_hbm, h1, h2, h3, h4,
+        gout, r1, r2, r3, r4,
+        xbuf, gbuf, obuf, w1, w2, w3, w4,
+        sbuf, rbuf, hidden, slope, gpre, st1, st2, st3, st4,
+        w_sem, a_send, a_recv, d_send, d_recv, own_sem, p_send, p_recv, go,
+    ):
+        me_t = lax.axis_index("tensor")
+        me_d = lax.axis_index("dp")
+        me_s = lax.axis_index("pipe")
+        me = me_t * nd + me_d
+        is_last = me_s == ns - 1
+        not_last = me_s < ns - 1
+        not_first = me_s > 0
+
+        def loop(start, stop, step):
+            def run(k, carry):
+                step(k)
+                return carry
+
+            lax.fori_loop(start, stop, run, 0)
+
+        mine = pl.ds(me_d * nb, nb)
+        loads = [
+            pltpu.make_async_copy(source.at[mine], held, w_sem.at[n])
+            for n, (source, held) in enumerate(((h1, w1), (h2, w2), (h3, w3), (h4, w4)))
+        ]
+        for n in (3, 0, 1, 2):
+            loads[n].start()
+
+        def member(k):
+            peer = lax.rem(me + k, group)
+            return peer, {"tensor": lax.div(peer, nd), "dp": lax.rem(peer, nd)}
+
+        barrier = pltpu.get_barrier_semaphore()
+
+        def greet(k):
+            pl.semaphore_signal(barrier, inc=1, device_id=member(k)[1], device_id_type=MESH)
+
+        loop(1, group, greet)
+        for k in range(1, ns):
+            pl.semaphore_signal(
+                barrier, inc=1, device_id={"pipe": lax.rem(me_s + k, ns)}, device_id_type=MESH
+            )
+        pl.semaphore_wait(barrier, group - 1 + ns - 1)
+
+        def wide_cols(d):
+            return pl.ds(pl.multiple_of(d * wide, wide), wide)
+
+        def cols(u):
+            return pl.ds(u * bs, bs)
+
+        def source_of(which, d):
+            if which == 0:
+                return x_hbm.at[:, wide_cols(d)]
+            if which == 1:
+                return cot_hbm.at[:, wide_cols(d)]
+            return (st1, st2, st3, st4, obuf)[which - 2].at[d]
+
+        def target_of(which):
+            if which == 6:
+                return gout.at[:, wide_cols(me_d)]
+            return (xbuf, gbuf, r1, r2, r3, r4)[which].at[me_d]
+
+        def share(which, k):
+            peer = lax.rem(me_d + k, nd)
+            return pltpu.make_async_remote_copy(
+                src_ref=source_of(which, peer),
+                dst_ref=target_of(which),
+                send_sem=d_send.at[which, k],
+                recv_sem=d_recv.at[which, k],
+                device_id={"dp": peer},
+                device_id_type=MESH,
+            )
+
+        def own(which):
+            return pltpu.make_async_copy(
+                source_of(which, me_d), target_of(which), own_sem.at[which]
+            )
+
+        def spread(which):
+            for k in range(1, nd):
+                share(which, k).start()
+            own(which).start()
+
+        def gathered(which):
+            own(which).wait()
+            for k in range(1, nd):
+                share(which, k).wait_recv()
+
+        def a2a(which, k):
+            peer, where = member(k)
+            return pltpu.make_async_remote_copy(
+                src_ref=sbuf.at[which, peer],
+                dst_ref=rbuf.at[which, me],
+                send_sem=a_send.at[which, k],
+                recv_sem=a_recv.at[which, k],
+                device_id=where,
+                device_id_type=MESH,
+            )
+
+        def send(which):
+            loop(1, group, lambda k: a2a(which, k).start())
+            rbuf[which, me] = sbuf[which, me]
+
+        def arrive(which):
+            loop(1, group, lambda k: a2a(which, k).wait_recv())
+
+        def produce(which, make):
+            parts = [make(u).reshape(group, nb, stride, total) for u in range(nb)]
+            sbuf[which] = jnp.concatenate(parts, axis=2).astype(bf16)
+
+        def block(which, j):
+            return rbuf[which, :, j].reshape(bs, total)
+
+        def tokens_of(ref, u):
+            return ref[:, :, cols(u)].reshape(total, bs)
+
+        def hand_on():
+            return pltpu.make_async_remote_copy(
+                src_ref=obuf,
+                dst_ref=gbuf,
+                send_sem=p_send,
+                recv_sem=p_recv,
+                device_id={"pipe": lax.rem(me_s + ns - 1, ns)},
+                device_id_type=MESH,
+            )
+
+        def make_first(u):
+            return mm(w1[u], tokens_of(xbuf, u), 0, 1)
+
+        def make_grad_last(u):
+            return mm(w4[u], tokens_of(gbuf, u), 1, 1)
+
+        def make_down(u):
+            return mm(w3[u], hidden[u], 0, 0)
+
+        def make_grad_mixed(u):
+            return mm(w2[u], gpre[u], 1, 0)
+
+        def piece(n):
+            return lax.div(n, pieces), pl.ds(pl.multiple_of(lax.rem(n, pieces) * bs, bs), bs)
+
+        @pl.when(is_last)
+        def _():
+            spread(1)
+
+        spread(0)
+        loads[3].wait()
+        loads[0].wait()
+
+        @pl.when(is_last)
+        def _():
+            gathered(1)
+            produce(1, make_grad_last)
+            send(1)
+
+        gathered(0)
+        produce(0, make_first)
+
+        @pl.when(not_last)
+        def _():
+            pl.semaphore_wait(go, 1)
+
+        send(0)
+        loads[1].wait()
+        loads[2].wait()
+        arrive(0)
+
+        @pl.when(not_first)
+        def _():
+            pl.semaphore_signal(go, inc=1, device_id={"pipe": me_s - 1}, device_id_type=MESH)
+
+        def forward(n):
+            u, part = piece(n)
+            pre = mm(w2[u, :, part], block(0, u), 0, 0)
+            cumulative = 0.5 * (1.0 + lax.erf(pre * root_half))
+            hidden[u, part] = (pre * cumulative).astype(bf16)
+            slope[u, part] = cumulative + pre * jnp.exp(-0.5 * pre * pre) * norm_density
+
+        loop(0, nb * pieces, forward)
+
+        @pl.when(not_last)
+        def _():
+            produce(2, make_down)
+            send(2)
+            hand_on().wait_recv()
+            produce(1, make_grad_last)
+            send(1)
+
+        arrive(1)
+
+        def backward(n):
+            u, part = piece(n)
+            gpre[u, part] = (mm(w3[u, part], block(1, u), 1, 0) * slope[u, part]).astype(bf16)
+
+        loop(0, nb * pieces, backward)
+        produce(3, make_grad_mixed)
+        send(3)
+
+        @pl.when(is_last)
+        def _():
+            produce(2, make_down)
+            send(2)
+
+        def scaled(value, out_rows):
+            return (value * factor).astype(bf16).reshape(nd, out_rows // nd, value.shape[1])
+
+        for u in range(nb):
+            st2[:, u] = scaled(mm(block(0, u), gpre[u], 1, 1), bs)
+        spread(3)
+        for u in range(nb):
+            st3[:, u] = scaled(mm(hidden[u], block(1, u), 1, 1), hb)
+        spread(4)
+
+        arrive(3)
+        for u in range(nb):
+            acts = mm(block(3, u), w1[u], 0, 1)
+            fresh = tokens_of(gbuf, u).astype(f32) + acts
+            obuf[:, :, cols(u)] = fresh.astype(bf16).reshape(nd, tokens, bs)
+
+        @pl.when(not_first)
+        def _():
+            hand_on().start()
+
+        spread(6)
+        for u in range(nb):
+            st1[:, u] = scaled(mm(tokens_of(xbuf, u).T, block(3, u), 1, 1), bs)
+        spread(2)
+        arrive(2)
+        for u in range(nb):
+            st4[:, u] = scaled(mm(block(2, u), tokens_of(gbuf, u), 1, 0), bs)
+        spread(5)
+
+        for which in range(4):
+            loop(1, group, lambda k: a2a(which, k).wait_send())
+        for k in range(1, nd):
+            share(0, k).wait_send()
+
+        @pl.when(is_last)
+        def _():
+            for k in range(1, nd):
+                share(1, k).wait_send()
+
+        for which in range(2, 7):
+            own(which).wait()
+            for k in range(1, nd):
+                share(which, k).wait()
+
+        @pl.when(not_first)
+        def _():
+            hand_on().wait_send()
+
+    return kernel
+
+
+def blocks_split(inputs, cotangent, up_first, up_second, down_first, down_second):
+    nt, nd, ns = (lax.axis_size(a) for a in ("tensor", "dp", "pipe"))
+    tokens, width = cotangent.shape
+    lb, bs, hb = up_second.shape[1:]
+    nb = lb // nd
+    total = nd * tokens
+    factor = 1.0 / math.sqrt(total)
+    anywhere = pl.BlockSpec(memory_space=pl.ANY)
+    shapes = (
+        (nd, nb, bs // nd, bs),
+        (nd, nb, bs // nd, hb),
+        (nd, nb, hb // nd, bs),
+        (nd, nb, bs // nd, bs),
+    )
+    group = nt * nd
+    exchange = (4, group, nb, bs // group, total)
+    dma = pltpu.SemaphoreType.DMA
+    flops = 2 * total * nb * bs * (8 * bs + 10 * hb)
+    out = pl.pallas_call(
+        make_block_kernel((nt, nd, ns, nb, bs, hb, tokens), factor),
+        out_shape=(jax.ShapeDtypeStruct((tokens, width), bf16),)
+        + tuple(jax.ShapeDtypeStruct(s, bf16) for s in shapes),
+        in_specs=[anywhere] * 6,
+        out_specs=(anywhere,) * 5,
+        scratch_shapes=[pltpu.VMEM((nd, tokens, nb * bs), bf16)] * 3
+        + [
+            pltpu.VMEM((nb, bs, bs), bf16),
+            pltpu.VMEM((nb, bs, hb), bf16),
+            pltpu.VMEM((nb, hb, bs), bf16),
+            pltpu.VMEM((nb, bs, bs), bf16),
+            pltpu.VMEM(exchange, bf16),
+            pltpu.VMEM(exchange, bf16),
+            pltpu.VMEM((nb, hb, total), bf16),
+            pltpu.VMEM((nb, hb, total), f32),
+            pltpu.VMEM((nb, hb, total), bf16),
+        ]
+        + [pltpu.VMEM(s, bf16) for s in shapes]
+        + [
+            dma((4,)),
+            dma((4, group)),
+            dma((4, group)),
+            dma((7, nd)),
+            dma((7, nd)),
+            dma((7,)),
+            dma,
+            dma,
+            pltpu.SemaphoreType.REGULAR,
+        ],
+        compiler_params=pltpu.CompilerParams(
+            collective_id=1, has_side_effects=True, vmem_limit_bytes=60 * 1024 * 1024
+        ),
+        cost_estimate=pl.CostEstimate(
+            flops=flops, bytes_accessed=8 * lb * bs * hb, transcendentals=2 * nb * hb * total
+        ),
+    )(inputs[0], cotangent, up_first[0], up_second[0], down_first[0], down_second[0])
+    grads = tuple(
+        part.reshape((lb,) + part.shape[2:]).astype(f32)[None] for part in out[1:]
+    )
+    return (out[0][None],) + grads
+
+
+def body(inputs, cotangent, up_first, up_second, down_first, down_second):
+    arrays = (inputs, cotangent, up_first, up_second, down_first, down_second)
+    nd = lax.axis_size("dp")
+    tokens = cotangent.shape[0]
+    stride = up_first.shape[-1] // (up_first.shape[1] * lax.axis_size("tensor"))
+    nb = up_first.shape[1] // nd
+    divides = up_first.shape[1] % nd == 0 and nb * stride % 16 == 0 and nb > 0
+    if divides and tokens % 16 == 0 and tokens * nd % lanes == 0:
+        return blocks_split(*arrays)
+    return tokens_split(*arrays)
+
+
 def solution(mesh):
     return jax.shard_map(
         body,

time: 194 us -> 131 us (0.68); the launches traced: 190 us -> 130 us
  Pallas kernels: 175 us -> 123 us
  local copies, waits for them, and re-layouts: 6.91 us -> 0.93 us
  other arithmetic: 7.43 us -> 5.33 us
    pallas_call x1, Pallas kernels: 175 us -> 123 us  [blocks_split(): pl.pallas_call(make_block_kernel((nt, nd, ns, nb, bs, hb, tokens), factor...]
    reduce_sum x3 -> x0, other arithmetic: 7.43 us -> none  [body(): sums = tuple((jnp.sum(part.astype(f32), axis=0)[None] for part in out[1:]))]
    convert_element_type x0 -> x3, other arithmetic: none -> 5.33 us  [blocks_split(): part.reshape((lb,) + part.shape[2:]).astype(f32)[None]]
    pad x2 -> x0, local copies, waits for them, and re-layouts: 4.55 us -> none  [the longest x1 2.28 us: body(): jnp.pad(inputs[0], pad)]
    broadcast_in_dim x1 -> x0, local copies, waits for them, and re-layouts: 2.35 us -> none  [body(): return (out[0][None, :tokens],) + sums]
where the time goes in v2:
time: 131 us; the launch traced here: 130 us
  Pallas kernels  123 us (94%)
  other arithmetic  5.33 us (4%)
    pallas_call x1, Pallas kernels, blocks_split(): pl.pallas_call(make_block_kernel((nt, nd, ns, nb, bs, hb, tokens), factor...  123 us
    convert_element_type x3, other arithmetic, blocks_split(): part.reshape((lb,) + part.shape[2:]).astype(f32)[None]  5.33 us

profile of v2, /device:TPU:0, one launch (start us, length us, event | category | flops | bytes accessed | tf_op | source)
XLA Modules:
  0.0 129.9 jit_solution(7773234414085949287)
XLA Ops:
  0.6 123.0 %shard_map.101 = (bf16[224,2048]{1,0:T(8,128)(2,1)}, bf16[4,2,64,256]{3,2,1,0:T(8,128)(2,1)}, bf16[4,2,64,1024]{3,2,1,0:T(8,128)(2,1)}, bf16[4,2,256,256]{3,2,1,0:T(8,128)(2,1)}, bf16[4,2,64,256]{3,2,1,0:T(8,128)(2,1)}) custom-call(bf16[224,2048]{1,0:T(8,128)(2,1)} %bitcast.30, bf16[224,2048]{1,0:T(8,128)(2,1)} %cot_hbm.1, bf16[8,256,256]{2,1,0:T(8,128)(2,1)} %bitcast.28, ...), custom_call_target="tpu_custom_call" | custom-call | flops 11274289152 | bytes 16777216 | tf_op jit(solution)/shard_map/pallas_call | solution.py:582
  123.7 0.0 copy-start.1
  123.7 0.0 copy-start
  123.7 2.3 %bitcast_convert_fusion.2 = (f32[1,8,64,256]{3,2,1,0:T(8,128)}, f32[1,8,64,256]{3,2,1,0:T(8,128)}) fusion(bf16[1,8,64,256]{3,2,1,0:T(8,128)(2,1)} %bitcast.25, bf16[1,8,64,256]{3,2,1,0:T(8,128)(2,1)} %bitcast.24), kind=kLoop, calls=%fused_computation.2 | loop fusion | flops 262144 | bytes 1572864 | tf_op jit(solution)/shard_map/convert_element_type | solution.py:620
  125.9 0.0 copy-done.1
  125.9 1.6 %bitcast_convert_fusion.1 = f32[1,8,64,1024]{3,2,1,0:T(8,128)} fusion(bf16[1,8,64,1024]{3,2,1,0:T(8,128)(2,1)S(1)} %bitcast.22), kind=kLoop, calls=%fused_computation.1 | loop fusion | flops 524288 | bytes 3145728 | tf_op jit(solution)/shard_map/convert_element_type | solution.py:620
  127.5 0.0 copy-done
  127.5 0.0 copy-start.2
  127.5 1.5 %bitcast_convert_fusion = f32[1,8,256,256]{3,2,1,0:T(8,128)} fusion(bf16[1,8,256,256]{3,2,1,0:T(8,128)(2,1)S(1)} %bitcast.21), kind=kLoop, calls=%fused_computation | loop fusion | flops 524288 | bytes 3145728 | tf_op jit(solution)/shard_map/convert_element_type | solution.py:620
  129.0 0.0 copy-done.2
  129.0 0.9 copy.12
Async XLA Ops:
  123.7 2.3 %copy-start.1 = (bf16[4,2,64,1024]{3,2,1,0:T(8,128)(2,1)S(1)}, bf16[4,2,64,1024]{3,2,1,0:T(8,128)(2,1)}, u32[]{:S(2)}) copy-start(bf16[4,2,64,1024]{3,2,1,0:T(8,128)(2,1)} %get-tuple-element.12) | copy-start | bytes 3145732
  123.7 3.8 %copy-start = (bf16[4,2,256,256]{3,2,1,0:T(8,128)(2,1)S(1)}, bf16[4,2,256,256]{3,2,1,0:T(8,128)(2,1)}, u32[]{:S(2)}) copy-start(bf16[4,2,256,256]{3,2,1,0:T(8,128)(2,1)} %get-tuple-element.13) | copy-start | bytes 3145732
  127.5 1.5 %copy-start.2 = (bf16[224,2048]{1,0:T(8,128)(2,1)S(1)}, bf16[224,2048]{1,0:T(8,128)(2,1)}, u32[]{:S(2)}) copy-start(bf16[224,2048]{1,0:T(8,128)(2,1)} %get-tuple-element.10) | copy-start | bytes 2752516

commit v3 on v2

--- a/solution.py
+++ b/solution.py
@@ -319,6 +319,7 @@
         is_last = me_s == ns - 1
         not_last = me_s < ns - 1
         not_first = me_s > 0
+        is_first = me_s == 0
 
         def loop(start, stop, step):
             def run(k, carry):
@@ -332,7 +333,7 @@
             pltpu.make_async_copy(source.at[mine], held, w_sem.at[n])
             for n, (source, held) in enumerate(((h1, w1), (h2, w2), (h3, w3), (h4, w4)))
         ]
-        for n in (3, 0, 1, 2):
+        for n in (0, 3, 1, 2):
             loads[n].start()
 
         def member(k):
@@ -448,35 +449,70 @@
         def piece(n):
             return lax.div(n, pieces), pl.ds(pl.multiple_of(lax.rem(n, pieces) * bs, bs), bs)
 
+        def tell(which, step):
+            pl.semaphore_signal(
+                go.at[which], inc=1, device_id={"pipe": me_s + step}, device_id_type=MESH
+            )
+
+        def scaled(value, out_rows):
+            return (value * factor).astype(bf16).reshape(nd, out_rows // nd, value.shape[1])
+
+        def finish_first():
+            for u in range(nb):
+                st1[:, u] = scaled(mm(tokens_of(xbuf, u).T, block(3, u), 1, 1), bs)
+
+        def finish_second():
+            for u in range(nb):
+                st2[:, u] = scaled(mm(block(0, u), gpre[u], 1, 1), bs)
+
+        def finish_down():
+            for u in range(nb):
+                st3[:, u] = scaled(mm(hidden[u], block(1, u), 1, 1), hb)
+
+        def finish_last():
+            for u in range(nb):
+                st4[:, u] = scaled(mm(block(2, u), tokens_of(gbuf, u), 1, 0), bs)
+
+        @pl.when(not_last)
+        def _():
+            pl.semaphore_wait(go.at[0], 1)
+
+        spread(0)
+
         @pl.when(is_last)
         def _():
             spread(1)
 
-        spread(0)
-        loads[3].wait()
         loads[0].wait()
-
-        @pl.when(is_last)
-        def _():
-            gathered(1)
-            produce(1, make_grad_last)
-            send(1)
-
         gathered(0)
         produce(0, make_first)
+        loads[3].wait()
 
         @pl.when(not_last)
         def _():
-            pl.semaphore_wait(go, 1)
+            pl.semaphore_wait(go.at[1], 1)
 
         send(0)
+
+        @pl.when(is_last)
+        def _():
+            gathered(1)
+
+        @pl.when(not_first)
+        def _():
+            tell(0, -1)
+
+        @pl.when(is_last)
+        def _():
+            produce(1, make_grad_last)
+
         loads[1].wait()
         loads[2].wait()
         arrive(0)
 
-        @pl.when(not_first)
-        def _():
-            pl.semaphore_signal(go, inc=1, device_id={"pipe": me_s - 1}, device_id_type=MESH)
+        @pl.when(is_last)
+        def _():
+            send(1)
 
         def forward(n):
             u, part = piece(n)
@@ -490,12 +526,29 @@
         @pl.when(not_last)
         def _():
             produce(2, make_down)
+            pl.semaphore_wait(go.at[2], 1)
             send(2)
             hand_on().wait_recv()
             produce(1, make_grad_last)
             send(1)
+            arrive(2)
+            finish_last()
+            spread(5)
 
         arrive(1)
+
+        @pl.when(not_first)
+        def _():
+            tell(1, -1)
+
+        @pl.when(not_last)
+        def _():
+            tell(3, 1)
+
+        @pl.when(is_first)
+        def _():
+            finish_down()
+            spread(4)
 
         def backward(n):
             u, part = piece(n)
@@ -504,23 +557,26 @@
         loop(0, nb * pieces, backward)
         produce(3, make_grad_mixed)
         send(3)
+        finish_second()
+
+        @pl.when(is_first)
+        def _():
+            spread(3)
+
+        @pl.when(not_first)
+        def _():
+            finish_down()
 
         @pl.when(is_last)
         def _():
             produce(2, make_down)
-            send(2)
-
-        def scaled(value, out_rows):
-            return (value * factor).astype(bf16).reshape(nd, out_rows // nd, value.shape[1])
-
-        for u in range(nb):
-            st2[:, u] = scaled(mm(block(0, u), gpre[u], 1, 1), bs)
-        spread(3)
-        for u in range(nb):
-            st3[:, u] = scaled(mm(hidden[u], block(1, u), 1, 1), hb)
-        spread(4)
 
         arrive(3)
+
+        @pl.when(not_first)
+        def _():
+            tell(2, -1)
+
         for u in range(nb):
             acts = mm(block(3, u), w1[u], 0, 1)
             fresh = tokens_of(gbuf, u).astype(f32) + acts
@@ -529,15 +585,23 @@
         @pl.when(not_first)
         def _():
             hand_on().start()
+            spread(3)
+            spread(4)
 
         spread(6)
-        for u in range(nb):
-            st1[:, u] = scaled(mm(tokens_of(xbuf, u).T, block(3, u), 1, 1), bs)
+        finish_first()
         spread(2)
-        arrive(2)
-        for u in range(nb):
-            st4[:, u] = scaled(mm(block(2, u), tokens_of(gbuf, u), 1, 0), bs)
-        spread(5)
+
+        @pl.when(not_first)
+        def _():
+            pl.semaphore_wait(go.at[3], 1)
+
+        @pl.when(is_last)
+        def _():
+            send(2)
+            arrive(2)
+            finish_last()
+            spread(5)
 
         for which in range(4):
             loop(1, group, lambda k: a2a(which, k).wait_send())
@@ -607,7 +671,7 @@
             dma((7,)),
             dma,
             dma,
-            pltpu.SemaphoreType.REGULAR,
+            pltpu.SemaphoreType.REGULAR((4,)),
         ],
         compiler_params=pltpu.CompilerParams(
             collective_id=1, has_side_effects=True, vmem_limit_bytes=60 * 1024 * 1024

time: 131 us -> 127 us (0.969)
  Pallas kernels: 123 us -> 120 us
    pallas_call x1, Pallas kernels: 123 us -> 120 us  [blocks_split(): pl.pallas_call(make_block_kernel((nt, nd, ns, nb, bs, hb, tokens), factor...]
where the time goes in v3:
time: 127 us; the launch traced here: 126 us
  Pallas kernels  120 us (94%)
  other arithmetic  5.33 us (4%)
    pallas_call x1, Pallas kernels, blocks_split(): pl.pallas_call(make_block_kernel((nt, nd, ns, nb, bs, hb, tokens), factor...  120 us
    convert_element_type x3, other arithmetic, blocks_split(): part.reshape((lb,) + part.shape[2:]).astype(f32)[None]  5.33 us

profile of v3, /device:TPU:0, one launch (start us, length us, event | category | flops | bytes accessed | tf_op | source)
XLA Modules:
  0.0 126.5 jit_solution(13944512270958856774)
XLA Ops:
  0.6 119.6 %shard_map.101 = (bf16[224,2048]{1,0:T(8,128)(2,1)}, bf16[4,2,64,256]{3,2,1,0:T(8,128)(2,1)}, bf16[4,2,64,1024]{3,2,1,0:T(8,128)(2,1)}, bf16[4,2,256,256]{3,2,1,0:T(8,128)(2,1)}, bf16[4,2,64,256]{3,2,1,0:T(8,128)(2,1)}) custom-call(bf16[224,2048]{1,0:T(8,128)(2,1)} %bitcast.30, bf16[224,2048]{1,0:T(8,128)(2,1)} %cot_hbm.1, bf16[8,256,256]{2,1,0:T(8,128)(2,1)} %bitcast.28, ...), custom_call_target="tpu_custom_call" | custom-call | flops 11274289152 | bytes 16777216 | tf_op jit(solution)/shard_map/pallas_call | solution.py:646
  120.2 0.0 copy-start.1
  120.2 0.0 copy-start
  120.2 2.3 %bitcast_convert_fusion.2 = (f32[1,8,64,256]{3,2,1,0:T(8,128)}, f32[1,8,64,256]{3,2,1,0:T(8,128)}) fusion(bf16[1,8,64,256]{3,2,1,0:T(8,128)(2,1)} %bitcast.25, bf16[1,8,64,256]{3,2,1,0:T(8,128)(2,1)} %bitcast.24), kind=kLoop, calls=%fused_computation.2 | loop fusion | flops 262144 | bytes 1572864 | tf_op jit(solution)/shard_map/convert_element_type | solution.py:684
  122.5 0.0 copy-done.1
  122.5 1.6 %bitcast_convert_fusion.1 = f32[1,8,64,1024]{3,2,1,0:T(8,128)} fusion(bf16[1,8,64,1024]{3,2,1,0:T(8,128)(2,1)S(1)} %bitcast.22), kind=kLoop, calls=%fused_computation.1 | loop fusion | flops 524288 | bytes 3145728 | tf_op jit(solution)/shard_map/convert_element_type | solution.py:684
  124.0 0.0 copy-done
  124.0 0.0 copy-start.2
  124.0 1.5 %bitcast_convert_fusion = f32[1,8,256,256]{3,2,1,0:T(8,128)} fusion(bf16[1,8,256,256]{3,2,1,0:T(8,128)(2,1)S(1)} %bitcast.21), kind=kLoop, calls=%fused_computation | loop fusion | flops 524288 | bytes 3145728 | tf_op jit(solution)/shard_map/convert_element_type | solution.py:684
  125.6 0.0 copy-done.2
  125.6 0.9 copy.12
Async XLA Ops:
  120.2 2.3 %copy-start.1 = (bf16[4,2,64,1024]{3,2,1,0:T(8,128)(2,1)S(1)}, bf16[4,2,64,1024]{3,2,1,0:T(8,128)(2,1)}, u32[]{:S(2)}) copy-start(bf16[4,2,64,1024]{3,2,1,0:T(8,128)(2,1)} %get-tuple-element.12) | copy-start | bytes 3145732
  120.2 3.8 %copy-start = (bf16[4,2,256,256]{3,2,1,0:T(8,128)(2,1)S(1)}, bf16[4,2,256,256]{3,2,1,0:T(8,128)(2,1)}, u32[]{:S(2)}) copy-start(bf16[4,2,256,256]{3,2,1,0:T(8,128)(2,1)} %get-tuple-element.13) | copy-start | bytes 3145732
  124.0 1.5 %copy-start.2 = (bf16[224,2048]{1,0:T(8,128)(2,1)S(1)}, bf16[224,2048]{1,0:T(8,128)(2,1)}, u32[]{:S(2)}) copy-start(bf16[224,2048]{1,0:T(8,128)(2,1)} %get-tuple-element.10) | copy-start | bytes 2752516

commit v4 on v3

--- a/solution.py
+++ b/solution.py
@@ -11,6 +11,7 @@
 root_half = 1.0 / math.sqrt(2.0)
 norm_density = 1.0 / math.sqrt(2.0 * math.pi)
 lanes = 128
+tile = 16
 f32 = jnp.float32
 bf16 = jnp.bfloat16
 
@@ -516,10 +517,17 @@
 
         def forward(n):
             u, part = piece(n)
-            pre = mm(w2[u, :, part], block(0, u), 0, 0)
-            cumulative = 0.5 * (1.0 + lax.erf(pre * root_half))
-            hidden[u, part] = (pre * cumulative).astype(bf16)
-            slope[u, part] = cumulative + pre * jnp.exp(-0.5 * pre * pre) * norm_density
+            slope[u, part] = mm(w2[u, :, part], block(0, u), 0, 0)
+            start = lax.rem(n, pieces) * bs
+
+            def activate(m):
+                at = pl.ds(pl.multiple_of(start + m * tile, tile), tile)
+                pre = slope[u, at]
+                cumulative = 0.5 + 0.5 * lax.erf(pre * root_half)
+                hidden[u, at] = (pre * cumulative).astype(bf16)
+                slope[u, at] = cumulative + pre * jnp.exp(-0.5 * pre * pre) * norm_density
+
+            loop(0, bs // tile, activate)
 
         loop(0, nb * pieces, forward)
 

time: 127 us -> 127 us (level)
  no operation moved by 1% of the time
where the time goes in v4:
time: 127 us
  Pallas kernels  120 us (94%)
  other arithmetic  5.33 us (4%)
    pallas_call x1, Pallas kernels, blocks_split(): pl.pallas_call(make_block_kernel((nt, nd, ns, nb, bs, hb, tokens), factor...  120 us
    convert_element_type x3, other arithmetic, blocks_split(): part.reshape((lb,) + part.shape[2:]).astype(f32)[None]  5.33 us

profile of v4, /device:TPU:0, one launch (start us, length us, event | category | flops | bytes accessed | tf_op | source)
XLA Modules:
  0.0 126.7 jit_solution(5770657923832943515)
XLA Ops:
  0.6 119.8 %shard_map.101 = (bf16[224,2048]{1,0:T(8,128)(2,1)}, bf16[4,2,64,256]{3,2,1,0:T(8,128)(2,1)}, bf16[4,2,64,1024]{3,2,1,0:T(8,128)(2,1)}, bf16[4,2,256,256]{3,2,1,0:T(8,128)(2,1)}, bf16[4,2,64,256]{3,2,1,0:T(8,128)(2,1)}) custom-call(bf16[224,2048]{1,0:T(8,128)(2,1)} %bitcast.30, bf16[224,2048]{1,0:T(8,128)(2,1)} %cot_hbm.1, bf16[8,256,256]{2,1,0:T(8,128)(2,1)} %bitcast.28, ...), custom_call_target="tpu_custom_call" | custom-call | flops 11274289152 | bytes 16777216 | tf_op jit(solution)/shard_map/pallas_call | solution.py:654
  120.4 0.0 copy-start.1
  120.4 0.0 copy-start
  120.4 2.3 %bitcast_convert_fusion.2 = (f32[1,8,64,256]{3,2,1,0:T(8,128)}, f32[1,8,64,256]{3,2,1,0:T(8,128)}) fusion(bf16[1,8,64,256]{3,2,1,0:T(8,128)(2,1)} %bitcast.25, bf16[1,8,64,256]{3,2,1,0:T(8,128)(2,1)} %bitcast.24), kind=kLoop, calls=%fused_computation.2 | loop fusion | flops 262144 | bytes 1572864 | tf_op jit(solution)/shard_map/convert_element_type | solution.py:692
  122.7 0.0 copy-done.1
  122.7 1.6 %bitcast_convert_fusion.1 = f32[1,8,64,1024]{3,2,1,0:T(8,128)} fusion(bf16[1,8,64,1024]{3,2,1,0:T(8,128)(2,1)S(1)} %bitcast.22), kind=kLoop, calls=%fused_computation.1 | loop fusion | flops 524288 | bytes 3145728 | tf_op jit(solution)/shard_map/convert_element_type | solution.py:692
  124.2 0.0 copy-done
  124.3 0.0 copy-start.2
  124.3 1.5 %bitcast_convert_fusion = f32[1,8,256,256]{3,2,1,0:T(8,128)} fusion(bf16[1,8,256,256]{3,2,1,0:T(8,128)(2,1)S(1)} %bitcast.21), kind=kLoop, calls=%fused_computation | loop fusion | flops 524288 | bytes 3145728 | tf_op jit(solution)/shard_map/convert_element_type | solution.py:692
  125.8 0.0 copy-done.2
  125.8 0.9 copy.12
Async XLA Ops:
  120.4 2.3 %copy-start.1 = (bf16[4,2,64,1024]{3,2,1,0:T(8,128)(2,1)S(1)}, bf16[4,2,64,1024]{3,2,1,0:T(8,128)(2,1)}, u32[]{:S(2)}) copy-start(bf16[4,2,64,1024]{3,2,1,0:T(8,128)(2,1)} %get-tuple-element.12) | copy-start | bytes 3145732
  120.4 3.8 %copy-start = (bf16[4,2,256,256]{3,2,1,0:T(8,128)(2,1)S(1)}, bf16[4,2,256,256]{3,2,1,0:T(8,128)(2,1)}, u32[]{:S(2)}) copy-start(bf16[4,2,256,256]{3,2,1,0:T(8,128)(2,1)} %get-tuple-element.13) | copy-start | bytes 3145732
  124.3 1.5 %copy-start.2 = (bf16[224,2048]{1,0:T(8,128)(2,1)S(1)}, bf16[224,2048]{1,0:T(8,128)(2,1)}, u32[]{:S(2)}) copy-start(bf16[224,2048]{1,0:T(8,128)(2,1)} %get-tuple-element.10) | copy-start | bytes 2752516

commit v5 on v3

--- a/solution.py
+++ b/solution.py
@@ -11,6 +11,7 @@
 root_half = 1.0 / math.sqrt(2.0)
 norm_density = 1.0 / math.sqrt(2.0 * math.pi)
 lanes = 128
+tile = 16
 f32 = jnp.float32
 bf16 = jnp.bfloat16
 
@@ -304,6 +305,9 @@
     total = nd * tokens
     wide = nb * bs
     pieces = hb // bs
+    cut = (total // lanes + 1) // 2 * lanes
+    spans = (pl.ds(0, cut), pl.ds(cut, total - cut))
+    halves = range(2)
 
     def kernel(
         x_hbm, cot_hbm, h1, h2, h3, h4,
@@ -355,6 +359,9 @@
         def wide_cols(d):
             return pl.ds(pl.multiple_of(d * wide, wide), wide)
 
+        def token_rows(d):
+            return pl.ds(pl.multiple_of(d * tokens, tile), tokens)
+
         def cols(u):
             return pl.ds(u * bs, bs)
 
@@ -363,12 +370,16 @@
                 return x_hbm.at[:, wide_cols(d)]
             if which == 1:
                 return cot_hbm.at[:, wide_cols(d)]
-            return (st1, st2, st3, st4, obuf)[which - 2].at[d]
+            if which == 6:
+                return obuf.at[token_rows(d)]
+            return (st1, st2, st3, st4)[which - 2].at[d]
 
         def target_of(which):
             if which == 6:
                 return gout.at[:, wide_cols(me_d)]
-            return (xbuf, gbuf, r1, r2, r3, r4)[which].at[me_d]
+            if which < 2:
+                return (xbuf, gbuf)[which].at[token_rows(me_d)]
+            return (r1, r2, r3, r4)[which - 2].at[me_d]
 
         def share(which, k):
             peer = lax.rem(me_d + k, nd)
@@ -396,55 +407,55 @@
             for k in range(1, nd):
                 share(which, k).wait_recv()
 
-        def a2a(which, k):
+        def a2a(which, h, k):
             peer, where = member(k)
             return pltpu.make_async_remote_copy(
-                src_ref=sbuf.at[which, peer],
-                dst_ref=rbuf.at[which, me],
-                send_sem=a_send.at[which, k],
-                recv_sem=a_recv.at[which, k],
+                src_ref=sbuf.at[which, peer, :, :, spans[h]],
+                dst_ref=rbuf.at[which, me, :, :, spans[h]],
+                send_sem=a_send.at[which, h, k],
+                recv_sem=a_recv.at[which, h, k],
                 device_id=where,
                 device_id_type=MESH,
             )
 
-        def send(which):
-            loop(1, group, lambda k: a2a(which, k).start())
-            rbuf[which, me] = sbuf[which, me]
-
-        def arrive(which):
-            loop(1, group, lambda k: a2a(which, k).wait_recv())
-
-        def produce(which, make):
-            parts = [make(u).reshape(group, nb, stride, total) for u in range(nb)]
-            sbuf[which] = jnp.concatenate(parts, axis=2).astype(bf16)
+        def send(which, h):
+            loop(1, group, lambda k: a2a(which, h, k).start())
+            rbuf[which, me, :, :, spans[h]] = sbuf[which, me, :, :, spans[h]]
+
+        def arrive(which, h):
+            loop(1, group, lambda k: a2a(which, h, k).wait_recv())
+
+        def produce(which, make, h):
+            parts = [make(u, h).reshape(group, nb, stride, spans[h].size) for u in range(nb)]
+            sbuf[which, :, :, :, spans[h]] = jnp.concatenate(parts, axis=2).astype(bf16)
 
         def block(which, j):
             return rbuf[which, :, j].reshape(bs, total)
 
-        def tokens_of(ref, u):
-            return ref[:, :, cols(u)].reshape(total, bs)
-
-        def hand_on():
+        def part_block(which, j, h):
+            return rbuf[which, :, j, :, spans[h]].reshape(bs, spans[h].size)
+
+        def hand_on(h):
             return pltpu.make_async_remote_copy(
-                src_ref=obuf,
-                dst_ref=gbuf,
-                send_sem=p_send,
-                recv_sem=p_recv,
+                src_ref=obuf.at[spans[h]],
+                dst_ref=gbuf.at[spans[h]],
+                send_sem=p_send.at[h],
+                recv_sem=p_recv.at[h],
                 device_id={"pipe": lax.rem(me_s + ns - 1, ns)},
                 device_id_type=MESH,
             )
 
-        def make_first(u):
-            return mm(w1[u], tokens_of(xbuf, u), 0, 1)
-
-        def make_grad_last(u):
-            return mm(w4[u], tokens_of(gbuf, u), 1, 1)
-
-        def make_down(u):
-            return mm(w3[u], hidden[u], 0, 0)
-
-        def make_grad_mixed(u):
-            return mm(w2[u], gpre[u], 1, 0)
+        def make_first(u, h):
+            return mm(w1[u], xbuf[spans[h], cols(u)], 0, 1)
+
+        def make_grad_last(u, h):
+            return mm(w4[u], gbuf[spans[h], cols(u)], 1, 1)
+
+        def make_down(u, h):
+            return mm(w3[u], hidden[u, :, spans[h]], 0, 0)
+
+        def make_grad_mixed(u, h):
+            return mm(w2[u], gpre[u, :, spans[h]], 1, 0)
 
         def piece(n):
             return lax.div(n, pieces), pl.ds(pl.multiple_of(lax.rem(n, pieces) * bs, bs), bs)
@@ -459,7 +470,7 @@
 
         def finish_first():
             for u in range(nb):
-                st1[:, u] = scaled(mm(tokens_of(xbuf, u).T, block(3, u), 1, 1), bs)
+                st1[:, u] = scaled(mm(xbuf[:, cols(u)].T, block(3, u), 1, 1), bs)
 
         def finish_second():
             for u in range(nb):
@@ -471,7 +482,7 @@
 
         def finish_last():
             for u in range(nb):
-                st4[:, u] = scaled(mm(block(2, u), tokens_of(gbuf, u), 1, 0), bs)
+                st4[:, u] = scaled(mm(block(2, u), gbuf[:, cols(u)], 1, 0), bs)
 
         @pl.when(not_last)
         def _():
@@ -482,111 +493,135 @@
         @pl.when(is_last)
         def _():
             spread(1)
+
+        def forward(h):
+            def one(n):
+                u, part = piece(n)
+                slope[u, part, spans[h]] = mm(w2[u, :, part], part_block(0, u, h), 0, 0)
+                start = lax.rem(n, pieces) * bs
+
+                def activate(m):
+                    at = pl.ds(pl.multiple_of(start + m * tile, tile), tile)
+                    pre = slope[u, at, spans[h]]
+                    cumulative = 0.5 + 0.5 * lax.erf(pre * root_half)
+                    hidden[u, at, spans[h]] = (pre * cumulative).astype(bf16)
+                    density = jnp.exp(-0.5 * pre * pre) * norm_density
+                    slope[u, at, spans[h]] = cumulative + pre * density
+
+                loop(0, bs // tile, activate)
+
+            loop(0, nb * pieces, one)
+
+        def backward(h):
+            def one(n):
+                u, part = piece(n)
+                grad_hidden = mm(w3[u, part], part_block(1, u, h), 1, 0)
+                gpre[u, part, spans[h]] = (grad_hidden * slope[u, part, spans[h]]).astype(bf16)
+
+            loop(0, nb * pieces, one)
+
+        def outgoing(h):
+            for u in range(nb):
+                acts = mm(part_block(3, u, h), w1[u], 0, 1)
+                fresh = gbuf[spans[h], cols(u)].astype(f32) + acts
+                obuf[spans[h], cols(u)] = fresh.astype(bf16)
 
         loads[0].wait()
         gathered(0)
-        produce(0, make_first)
+
+        @pl.when(not_last)
+        def _():
+            pl.semaphore_wait(go.at[1], 1)
+
+        for h in halves:
+            produce(0, make_first, h)
+            send(0, h)
+
+        @pl.when(is_last)
+        def _():
+            gathered(1)
+
+        @pl.when(not_first)
+        def _():
+            tell(0, -1)
+
         loads[3].wait()
 
-        @pl.when(not_last)
-        def _():
-            pl.semaphore_wait(go.at[1], 1)
-
-        send(0)
-
-        @pl.when(is_last)
-        def _():
-            gathered(1)
-
-        @pl.when(not_first)
-        def _():
-            tell(0, -1)
-
-        @pl.when(is_last)
-        def _():
-            produce(1, make_grad_last)
+        @pl.when(is_last)
+        def _():
+            for h in halves:
+                produce(1, make_grad_last, h)
 
         loads[1].wait()
         loads[2].wait()
-        arrive(0)
-
-        @pl.when(is_last)
-        def _():
-            send(1)
-
-        def forward(n):
-            u, part = piece(n)
-            pre = mm(w2[u, :, part], block(0, u), 0, 0)
-            cumulative = 0.5 * (1.0 + lax.erf(pre * root_half))
-            hidden[u, part] = (pre * cumulative).astype(bf16)
-            slope[u, part] = cumulative + pre * jnp.exp(-0.5 * pre * pre) * norm_density
-
-        loop(0, nb * pieces, forward)
+        arrive(0, 0)
+
+        @pl.when(is_last)
+        def _():
+            send(1, 0)
+
+        forward(0)
+        arrive(0, 1)
+
+        @pl.when(is_last)
+        def _():
+            send(1, 1)
 
         @pl.when(not_last)
         def _():
-            produce(2, make_down)
-            pl.semaphore_wait(go.at[2], 1)
-            send(2)
-            hand_on().wait_recv()
-            produce(1, make_grad_last)
-            send(1)
-            arrive(2)
+            forward(1)
+            for h in halves:
+                produce(2, make_down, h)
+                send(2, h)
+            for h in halves:
+                hand_on(h).wait_recv()
+                produce(1, make_grad_last, h)
+                send(1, h)
+
+        arrive(1, 0)
+        backward(0)
+        produce(3, make_grad_mixed, 0)
+        send(3, 0)
+
+        @pl.when(is_last)
+        def _():
+            forward(1)
+
+        arrive(1, 1)
+
+        @pl.when(not_first)
+        def _():
+            tell(1, -1)
+
+        @pl.when(not_last)
+        def _():
+            tell(2, 1)
+
+        backward(1)
+        produce(3, make_grad_mixed, 1)
+        send(3, 1)
+
+        @pl.when(is_first)
+        def _():
+            finish_down()
+            spread(4)
+            finish_second()
+            spread(3)
+
+        @pl.when(not_last)
+        def _():
+            for h in halves:
+                arrive(2, h)
             finish_last()
             spread(5)
 
-        arrive(1)
-
-        @pl.when(not_first)
-        def _():
-            tell(1, -1)
-
-        @pl.when(not_last)
-        def _():
-            tell(3, 1)
-
-        @pl.when(is_first)
-        def _():
-            finish_down()
-            spread(4)
-
-        def backward(n):
-            u, part = piece(n)
-            gpre[u, part] = (mm(w3[u, part], block(1, u), 1, 0) * slope[u, part]).astype(bf16)
-
-        loop(0, nb * pieces, backward)
-        produce(3, make_grad_mixed)
-        send(3)
-        finish_second()
-
-        @pl.when(is_first)
-        def _():
-            spread(3)
-
-        @pl.when(not_first)
-        def _():
-            finish_down()
-
-        @pl.when(is_last)
-        def _():
-            produce(2, make_down)
-
-        arrive(3)
-
-        @pl.when(not_first)
-        def _():
-            tell(2, -1)
-
-        for u in range(nb):
-            acts = mm(block(3, u), w1[u], 0, 1)
-            fresh = tokens_of(gbuf, u).astype(f32) + acts
-            obuf[:, :, cols(u)] = fresh.astype(bf16).reshape(nd, tokens, bs)
-
-        @pl.when(not_first)
-        def _():
-            hand_on().start()
-            spread(3)
-            spread(4)
+        for h in halves:
+            arrive(3, h)
+            outgoing(h)
+
+            @pl.when(not_first)
+            def _():
+                hand_on(h).start()
 
         spread(6)
         finish_first()
@@ -594,17 +629,32 @@
 
         @pl.when(not_first)
         def _():
-            pl.semaphore_wait(go.at[3], 1)
-
-        @pl.when(is_last)
-        def _():
-            send(2)
-            arrive(2)
+            finish_down()
+            spread(4)
+            finish_second()
+            spread(3)
+
+        @pl.when(is_last)
+        def _():
+            for h in halves:
+                produce(2, make_down, h)
+
+        @pl.when(not_first)
+        def _():
+            pl.semaphore_wait(go.at[2], 1)
+
+        @pl.when(is_last)
+        def _():
+            for h in halves:
+                send(2, h)
+            for h in halves:
+                arrive(2, h)
             finish_last()
             spread(5)
 
         for which in range(4):
-            loop(1, group, lambda k: a2a(which, k).wait_send())
+            for h in halves:
+                loop(1, group, lambda k: a2a(which, h, k).wait_send())
         for k in range(1, nd):
             share(0, k).wait_send()
 
@@ -620,7 +670,8 @@
 
         @pl.when(not_first)
         def _():
-            hand_on().wait_send()
+            for h in halves:
+                hand_on(h).wait_send()
 
     return kernel
 
@@ -649,7 +700,7 @@
         + tuple(jax.ShapeDtypeStruct(s, bf16) for s in shapes),
         in_specs=[anywhere] * 6,
         out_specs=(anywhere,) * 5,
-        scratch_shapes=[pltpu.VMEM((nd, tokens, nb * bs), bf16)] * 3
+        scratch_shapes=[pltpu.VMEM((total, nb * bs), bf16)] * 3
         + [
             pltpu.VMEM((nb, bs, bs), bf16),
             pltpu.VMEM((nb, bs, hb), bf16),
@@ -664,14 +715,14 @@
         + [pltpu.VMEM(s, bf16) for s in shapes]
         + [
             dma((4,)),
-            dma((4, group)),
-            dma((4, group)),
+            dma((4, 2, group)),
+            dma((4, 2, group)),
             dma((7, nd)),
             dma((7, nd)),
             dma((7,)),
-            dma,
-            dma,
-            pltpu.SemaphoreType.REGULAR((4,)),
+            dma((2,)),
+            dma((2,)),
+            pltpu.SemaphoreType.REGULAR((3,)),
         ],
         compiler_params=pltpu.CompilerParams(
             collective_id=1, has_side_effects=True, vmem_limit_bytes=60 * 1024 * 1024
@@ -693,7 +744,7 @@
     stride = up_first.shape[-1] // (up_first.shape[1] * lax.axis_size("tensor"))
     nb = up_first.shape[1] // nd
     divides = up_first.shape[1] % nd == 0 and nb * stride % 16 == 0 and nb > 0
-    if divides and tokens % 16 == 0 and tokens * nd % lanes == 0:
+    if divides and tokens % 16 == 0 and tokens * nd % lanes == 0 and tokens * nd > lanes:
         return blocks_split(*arrays)
     return tokens_split(*arrays)
 

time: 127 us -> 128 us (level)
    pallas_call x1, Pallas kernels: 120 us -> 121 us  [blocks_split(): pl.pallas_call(make_block_kernel((nt, nd, ns, nb, bs, hb, tokens), factor...]
where the time goes in v5:
time: 128 us
  Pallas kernels  121 us (95%)
  other arithmetic  5.33 us (4%)
    pallas_call x1, Pallas kernels, blocks_split(): pl.pallas_call(make_block_kernel((nt, nd, ns, nb, bs, hb, tokens), factor...  121 us
    convert_element_type x3, other arithmetic, blocks_split(): part.reshape((lb,) + part.shape[2:]).astype(f32)[None]  5.33 us

profile of v5, /device:TPU:0, one launch (start us, length us, event | category | flops | bytes accessed | tf_op | source)
XLA Modules:
  0.0 128.1 jit_solution(16054236844032311122)
XLA Ops:
  0.6 121.2 %shard_map.101 = (bf16[224,2048]{1,0:T(8,128)(2,1)}, bf16[4,2,64,256]{3,2,1,0:T(8,128)(2,1)}, bf16[4,2,64,1024]{3,2,1,0:T(8,128)(2,1)}, bf16[4,2,256,256]{3,2,1,0:T(8,128)(2,1)}, bf16[4,2,64,256]{3,2,1,0:T(8,128)(2,1)}) custom-call(bf16[224,2048]{1,0:T(8,128)(2,1)} %bitcast.30, bf16[224,2048]{1,0:T(8,128)(2,1)} %cot_hbm.1, bf16[8,256,256]{2,1,0:T(8,128)(2,1)} %bitcast.28, ...), custom_call_target="tpu_custom_call" | custom-call | flops 11274289152 | bytes 16777216 | tf_op jit(solution)/shard_map/pallas_call | solution.py:697
  121.8 0.0 copy-start.1
  121.8 0.0 copy-start
  121.8 2.3 %bitcast_convert_fusion.2 = (f32[1,8,64,256]{3,2,1,0:T(8,128)}, f32[1,8,64,256]{3,2,1,0:T(8,128)}) fusion(bf16[1,8,64,256]{3,2,1,0:T(8,128)(2,1)} %bitcast.25, bf16[1,8,64,256]{3,2,1,0:T(8,128)(2,1)} %bitcast.24), kind=kLoop, calls=%fused_computation.2 | loop fusion | flops 262144 | bytes 1572864 | tf_op jit(solution)/shard_map/convert_element_type | solution.py:735
  124.1 0.0 copy-done.1
  124.1 1.6 %bitcast_convert_fusion.1 = f32[1,8,64,1024]{3,2,1,0:T(8,128)} fusion(bf16[1,8,64,1024]{3,2,1,0:T(8,128)(2,1)S(1)} %bitcast.22), kind=kLoop, calls=%fused_computation.1 | loop fusion | flops 524288 | bytes 3145728 | tf_op jit(solution)/shard_map/convert_element_type | solution.py:735
  125.7 0.0 copy-done
  125.7 0.0 copy-start.2
  125.7 1.5 %bitcast_convert_fusion = f32[1,8,256,256]{3,2,1,0:T(8,128)} fusion(bf16[1,8,256,256]{3,2,1,0:T(8,128)(2,1)S(1)} %bitcast.21), kind=kLoop, calls=%fused_computation | loop fusion | flops 524288 | bytes 3145728 | tf_op jit(solution)/shard_map/convert_element_type | solution.py:735
  127.2 0.0 copy-done.2
  127.2 0.9 copy.12
Async XLA Ops:
  121.8 2.3 %copy-start.1 = (bf16[4,2,64,1024]{3,2,1,0:T(8,128)(2,1)S(1)}, bf16[4,2,64,1024]{3,2,1,0:T(8,128)(2,1)}, u32[]{:S(2)}) copy-start(bf16[4,2,64,1024]{3,2,1,0:T(8,128)(2,1)} %get-tuple-element.12) | copy-start | bytes 3145732
  121.8 3.8 %copy-start = (bf16[4,2,256,256]{3,2,1,0:T(8,128)(2,1)S(1)}, bf16[4,2,256,256]{3,2,1,0:T(8,128)(2,1)}, u32[]{:S(2)}) copy-start(bf16[4,2,256,256]{3,2,1,0:T(8,128)(2,1)} %get-tuple-element.13) | copy-start | bytes 3145732
  125.7 1.5 %copy-start.2 = (bf16[224,2048]{1,0:T(8,128)(2,1)S(1)}, bf16[224,2048]{1,0:T(8,128)(2,1)}, u32[]{:S(2)}) copy-start(bf16[224,2048]{1,0:T(8,128)(2,1)} %get-tuple-element.10) | copy-start | bytes 2752516

commit v6 on v5

--- a/solution.py
+++ b/solution.py
@@ -529,10 +529,6 @@
         loads[0].wait()
         gathered(0)
 
-        @pl.when(not_last)
-        def _():
-            pl.semaphore_wait(go.at[1], 1)
-
         for h in halves:
             produce(0, make_first, h)
             send(0, h)
@@ -571,12 +567,12 @@
         def _():
             forward(1)
             for h in halves:
-                produce(2, make_down, h)
-                send(2, h)
-            for h in halves:
                 hand_on(h).wait_recv()
                 produce(1, make_grad_last, h)
                 send(1, h)
+            for h in halves:
+                produce(2, make_down, h)
+                send(2, h)
 
         arrive(1, 0)
         backward(0)
@@ -589,13 +585,9 @@
 
         arrive(1, 1)
 
-        @pl.when(not_first)
-        def _():
-            tell(1, -1)
-
         @pl.when(not_last)
         def _():
-            tell(2, 1)
+            tell(1, 1)
 
         backward(1)
         produce(3, make_grad_mixed, 1)
@@ -641,7 +633,7 @@
 
         @pl.when(not_first)
         def _():
-            pl.semaphore_wait(go.at[2], 1)
+            pl.semaphore_wait(go.at[1], 1)
 
         @pl.when(is_last)
         def _():
@@ -722,7 +714,7 @@
             dma((7,)),
             dma((2,)),
             dma((2,)),
-            pltpu.SemaphoreType.REGULAR((3,)),
+            pltpu.SemaphoreType.REGULAR((2,)),
         ],
         compiler_params=pltpu.CompilerParams(
             collective_id=1, has_side_effects=True, vmem_limit_bytes=60 * 1024 * 1024

time: 128 us -> 124 us (0.969)
  Pallas kernels: 121 us -> 117 us
    pallas_call x1, Pallas kernels: 121 us -> 117 us  [blocks_split(): pl.pallas_call(make_block_kernel((nt, nd, ns, nb, bs, hb, tokens), factor...]
where the time goes in v6:
time: 124 us
  Pallas kernels  117 us (94%)
  other arithmetic  5.33 us (4%)
    pallas_call x1, Pallas kernels, blocks_split(): pl.pallas_call(make_block_kernel((nt, nd, ns, nb, bs, hb, tokens), factor...  117 us
    convert_element_type x3, other arithmetic, blocks_split(): part.reshape((lb,) + part.shape[2:]).astype(f32)[None]  5.33 us

profile of v6, /device:TPU:0, one launch (start us, length us, event | category | flops | bytes accessed | tf_op | source)
XLA Modules:
  0.0 123.7 jit_solution(4042737305522490990)
XLA Ops:
  0.6 116.8 %shard_map.101 = (bf16[224,2048]{1,0:T(8,128)(2,1)}, bf16[4,2,64,256]{3,2,1,0:T(8,128)(2,1)}, bf16[4,2,64,1024]{3,2,1,0:T(8,128)(2,1)}, bf16[4,2,256,256]{3,2,1,0:T(8,128)(2,1)}, bf16[4,2,64,256]{3,2,1,0:T(8,128)(2,1)}) custom-call(bf16[224,2048]{1,0:T(8,128)(2,1)} %bitcast.30, bf16[224,2048]{1,0:T(8,128)(2,1)} %cot_hbm.1, bf16[8,256,256]{2,1,0:T(8,128)(2,1)} %bitcast.28, ...), custom_call_target="tpu_custom_call" | custom-call | flops 11274289152 | bytes 16777216 | tf_op jit(solution)/shard_map/pallas_call | solution.py:689
  117.4 0.0 copy-start.1
  117.4 0.0 copy-start
  117.4 2.3 %bitcast_convert_fusion.2 = (f32[1,8,64,256]{3,2,1,0:T(8,128)}, f32[1,8,64,256]{3,2,1,0:T(8,128)}) fusion(bf16[1,8,64,256]{3,2,1,0:T(8,128)(2,1)} %bitcast.25, bf16[1,8,64,256]{3,2,1,0:T(8,128)(2,1)} %bitcast.24), kind=kLoop, calls=%fused_computation.2 | loop fusion | flops 262144 | bytes 1572864 | tf_op jit(solution)/shard_map/convert_element_type | solution.py:727
  119.7 0.0 copy-done.1
  119.7 1.6 %bitcast_convert_fusion.1 = f32[1,8,64,1024]{3,2,1,0:T(8,128)} fusion(bf16[1,8,64,1024]{3,2,1,0:T(8,128)(2,1)S(1)} %bitcast.22), kind=kLoop, calls=%fused_computation.1 | loop fusion | flops 524288 | bytes 3145728 | tf_op jit(solution)/shard_map/convert_element_type | solution.py:727
  121.2 0.0 copy-done
  121.3 0.0 copy-start.2
  121.3 1.5 %bitcast_convert_fusion = f32[1,8,256,256]{3,2,1,0:T(8,128)} fusion(bf16[1,8,256,256]{3,2,1,0:T(8,128)(2,1)S(1)} %bitcast.21), kind=kLoop, calls=%fused_computation | loop fusion | flops 524288 | bytes 3145728 | tf_op jit(solution)/shard_map/convert_element_type | solution.py:727
  122.8 0.0 copy-done.2
  122.8 0.9 copy.12
Async XLA Ops:
  117.4 2.3 %copy-start.1 = (bf16[4,2,64,1024]{3,2,1,0:T(8,128)(2,1)S(1)}, bf16[4,2,64,1024]{3,2,1,0:T(8,128)(2,1)}, u32[]{:S(2)}) copy-start(bf16[4,2,64,1024]{3,2,1,0:T(8,128)(2,1)} %get-tuple-element.12) | copy-start | bytes 3145732
  117.4 3.8 %copy-start = (bf16[4,2,256,256]{3,2,1,0:T(8,128)(2,1)S(1)}, bf16[4,2,256,256]{3,2,1,0:T(8,128)(2,1)}, u32[]{:S(2)}) copy-start(bf16[4,2,256,256]{3,2,1,0:T(8,128)(2,1)} %get-tuple-element.13) | copy-start | bytes 3145732
  121.3 1.5 %copy-start.2 = (bf16[224,2048]{1,0:T(8,128)(2,1)S(1)}, bf16[224,2048]{1,0:T(8,128)(2,1)}, u32[]{:S(2)}) copy-start(bf16[224,2048]{1,0:T(8,128)(2,1)} %get-tuple-element.10) | copy-start | bytes 2752516
